TPU v7x, 128 devices: a whole 4x4x4 slice. The times are simulated.
128 devices in a mesh: var: 2 (over z_lo), py: 8 (over x, z_hi), pz: 8 (over y, core).
Axes of the slice: x: 4, y: 4, z: 4 (z_hi: 2, z_lo: 2; z = z_hi * 2 + z_lo), core: 2. Of those that a mesh axis runs over, the one named last changes fastest.
Arguments:
- order_field: float32 [12, 256, 256, 256], P('var', 'py', 'pz'), may hold values from 0 to 1
- strains: float32 [24, 6], replicated, may hold values from -2.4 to 2.4
- variant_strain: int32 [24], replicated, may hold values from 0 to 23, each once
Outputs:
- order_next: float32 [12, 256, 256, 256], P('var', 'py', 'pz')
Inputs may be any that keep to these rules, and one draw needn't show every extreme that they name: `variant_strain`: each bank row appears once.
All inputs are finite; a program needn't handle non-finite values.
Results may differ from a plain program's by a relative error of at most 0.00026.
Values sent between devices are 32-bit elements; how exact they have to be, the bound alone decides.
No kernel may reach another device: no remote copies, remote signals or barrier semaphores. Data moves between devices by JAX's collectives and lax.ppermute only.
A program may use at most 192 MiB of HBM per device.

v0:
```python
import jax
import jax.numpy as jnp
from jax import lax
from jax.sharding import PartitionSpec as P

lame_first = 1.5
shear_mod = 1.0
relax_coef = 1.0 / 1.4
grad_coef = 0.5
mobility = 0.2
landau_cubic = 3.0
landau_quartic = 0.5
two_pi = 6.283185307179586
highest = lax.Precision.HIGHEST


def angle_tables(length):
    row_ids = jnp.arange(length, dtype=jnp.int32)[:, None]
    col_ids = jnp.arange(length, dtype=jnp.int32)[None, :]
    angles = (row_ids * col_ids % length).astype(jnp.float32) * (two_pi / length)
    return (jnp.cos(angles), jnp.sin(angles))


def material(strains, variant_strain, variants):
    bank_rows = strains.shape[0]
    picked = variant_strain[:variants]
    one_hot = (picked[:, None] == jnp.arange(bank_rows, dtype=jnp.int32)[None, :]).astype(
        jnp.float32
    )
    chosen = jnp.dot(one_hot, strains, precision=highest)
    row_one = jnp.stack([chosen[:, 0], chosen[:, 5], chosen[:, 4]], axis=1)
    row_two = jnp.stack([chosen[:, 5], chosen[:, 1], chosen[:, 3]], axis=1)
    row_three = jnp.stack([chosen[:, 4], chosen[:, 3], chosen[:, 2]], axis=1)
    eigen_strain = jnp.stack([row_one, row_two, row_three], axis=1)
    trace_sum = chosen[:, 0] + chosen[:, 1] + chosen[:, 2]
    stress = (
        lame_first * trace_sum[:, None, None] * jnp.eye(3, dtype=jnp.float32)[None]
        + 2.0 * shear_mod * eigen_strain
    )
    energy = jnp.einsum("pij,qij->pq", stress, eigen_strain, precision=highest)
    return (stress, energy)


def signed_wave(indices, grid_len):
    return jnp.where(indices >= grid_len // 2, indices - grid_len, indices).astype(jnp.float32)


def geometry(wave_z, wave_y, raw_x, x_len, grid_len):
    wave_x = raw_x * (float(grid_len) / float(x_len))
    squared_norm = wave_x * wave_x + wave_y * wave_y + wave_z * wave_z
    inverse_norm = lax.rsqrt(jnp.maximum(squared_norm, 1.0))
    unit_dir = (wave_x * inverse_norm, wave_y * inverse_norm, wave_z * inverse_norm)
    keep_mask = (
        jnp.where((wave_y == -(grid_len // 2)) | (raw_x == -(x_len // 2)), 0.0, 1.0)
        + 0.0 * squared_norm
    )
    wave_sq = squared_norm * (two_pi / grid_len) ** 2
    return (unit_dir, keep_mask, wave_sq)


def projections(stress_blk, unit_dir):
    traction = []
    for row_id in range(3):
        total_sum = stress_blk[:, row_id, 0][:, None, None, None] * unit_dir[0][None]
        for col_id in range(1, 3):
            total_sum = (
                total_sum
                + stress_blk[:, row_id, col_id][:, None, None, None] * unit_dir[col_id][None]
            )
        traction.append(total_sum)
    normal = (
        unit_dir[0][None] * traction[0]
        + unit_dir[1][None] * traction[1]
        + unit_dir[2][None] * traction[2]
    )
    return (traction, normal)


def shared_sums(traction, normal, spec_real, spec_imag):
    factors = [traction[0], traction[1], traction[2], normal]
    sum_real = jnp.stack([jnp.sum(factor * spec_real, axis=0) for factor in factors], axis=0)
    sum_imag = jnp.stack([jnp.sum(factor * spec_imag, axis=0) for factor in factors], axis=0)
    return (sum_real, sum_imag)


def mixing(coeffs, spec_real, spec_imag):
    mix_real = jnp.einsum("pq,qabc->pabc", coeffs, spec_real, precision=highest)
    mix_imag = jnp.einsum("pq,qabc->pabc", coeffs, spec_imag, precision=highest)
    return (mix_real, mix_imag)


def complex_section(pattern, real_part, imag_part, cos_table, sin_table, sign_value):
    real_cos = jnp.einsum(pattern, real_part, cos_table, precision=highest)
    real_sin = jnp.einsum(pattern, real_part, sin_table, precision=highest)
    imag_cos = jnp.einsum(pattern, imag_part, cos_table, precision=highest)
    imag_sin = jnp.einsum(pattern, imag_part, sin_table, precision=highest)
    return (real_cos - sign_value * imag_sin, imag_cos + sign_value * real_sin)


def shards(order_field, strains, variant_strain):
    own_count = order_field.shape[0]
    local_first = order_field.shape[1]
    local_second = order_field.shape[2]
    grid_len = order_field.shape[3]
    half_len = grid_len // 2
    cross_devs = lax.axis_size("py")
    depth_devs = lax.axis_size("pz")
    group_count = lax.axis_size("var")
    var_group = lax.axis_index("var")
    x_len = local_first * cross_devs
    block_cells = local_first * local_second
    stress, energy = material(strains, variant_strain, own_count * group_count)
    squares = jnp.sum(order_field * order_field, axis=0)
    total_sq = lax.psum(squares, "var")
    cos_full, sin_full = angle_tables(grid_len)
    cos_xdim, sin_xdim = angle_tables(x_len)
    cos_half = cos_full[:, :half_len]
    sin_half = sin_full[:, :half_len]
    weights = jnp.where(jnp.arange(half_len, dtype=jnp.int32) == 0, 1.0, 2.0)
    cos_back = cos_full[:half_len, :] * weights[:, None]
    sin_back = sin_full[:half_len, :] * weights[:, None]
    cos_ytab = cos_full.reshape(depth_devs, local_second, grid_len)
    sin_ytab = sin_full.reshape(depth_devs, local_second, grid_len)
    cos_xtab = cos_xdim.reshape(cross_devs, local_first, x_len)
    sin_xtab = sin_xdim.reshape(cross_devs, local_first, x_len)
    cos_yback = cos_full.reshape(grid_len, depth_devs, local_second)
    sin_yback = sin_full.reshape(grid_len, depth_devs, local_second)
    cos_xback = cos_xdim.reshape(x_len, cross_devs, local_first)
    sin_xback = sin_xdim.reshape(x_len, cross_devs, local_first)

    def to_planes(first_part, second_part):
        return (
            lax.all_to_all(first_part, ("py", "pz"), split_axis=1, concat_axis=1, tiled=True),
            lax.all_to_all(second_part, ("py", "pz"), split_axis=1, concat_axis=1, tiled=True),
        )

    flat_shape = (own_count, half_len, block_cells)
    spec_real = jnp.einsum("vxyz,zk->vkxy", order_field, cos_half, precision=highest).reshape(
        flat_shape
    )
    spec_imag = -jnp.einsum("vxyz,zk->vkxy", order_field, sin_half, precision=highest).reshape(
        flat_shape
    )
    wave_full = signed_wave(jnp.arange(grid_len, dtype=jnp.int32), grid_len)
    plane_count = half_len // (cross_devs * depth_devs)
    spec_real, spec_imag = to_planes(spec_real, spec_imag)
    shaped = (own_count, cross_devs, depth_devs, plane_count, local_first, local_second)
    spec_real, spec_imag = complex_section(
        "vacqxy,cyn->vaqxn",
        spec_real.reshape(shaped),
        spec_imag.reshape(shaped),
        cos_ytab,
        sin_ytab,
        -1.0,
    )
    spec_real, spec_imag = complex_section(
        "vaqxn,axm->vqmn", spec_real, spec_imag, cos_xtab, sin_xtab, -1.0
    )
    plane_id = lax.axis_index("py") * depth_devs + lax.axis_index("pz")
    wave_z = (plane_id * plane_count + jnp.arange(plane_count, dtype=jnp.int32)).astype(
        jnp.float32
    )[:, None, None]
    raw_x = signed_wave(jnp.arange(x_len, dtype=jnp.int32), x_len)[None, :, None]
    wave_y = wave_full[None, None, :]
    unit_dir, keep_mask, wave_sq = geometry(wave_z, wave_y, raw_x, x_len, grid_len)
    own_stress = lax.dynamic_slice_in_dim(stress, var_group * own_count, own_count, 0)
    traction_own, normal_own = projections(own_stress, unit_dir)
    shared_real, shared_imag = shared_sums(traction_own, normal_own, spec_real, spec_imag)
    columns = lax.dynamic_slice_in_dim(energy, var_group * own_count, own_count, 1)
    mix_real, mix_imag = mixing(columns, spec_real, spec_imag)
    mix_real, mix_imag = (
        lax.psum_scatter(mix_real, "var", scatter_dimension=0, tiled=True),
        lax.psum_scatter(mix_imag, "var", scatter_dimension=0, tiled=True),
    )
    shared_real, shared_imag = lax.psum((shared_real, shared_imag), "var")
    inverse_volume = 1.0 / float(x_len * grid_len * grid_len)

    def driving(mix_part, shared_part, own_part):
        relaxed = (
            traction_own[0] * shared_part[0][None]
            + traction_own[1] * shared_part[1][None]
            + traction_own[2] * shared_part[2][None]
            - relax_coef * normal_own * shared_part[3][None]
        )
        return (
            keep_mask[None]
            * (mix_part - relaxed / shear_mod + grad_coef * wave_sq[None] * own_part)
            * inverse_volume
        )

    resp_real = driving(mix_real, shared_real, spec_real)
    resp_imag = driving(mix_imag, shared_imag, spec_imag)
    resp_real, resp_imag = complex_section(
        "vqmn,max->vaqxn", resp_real, resp_imag, cos_xback, sin_xback, 1.0
    )
    resp_real, resp_imag = complex_section(
        "vaqxn,ncy->vacqxy", resp_real, resp_imag, cos_yback, sin_yback, 1.0
    )
    resp_real, resp_imag = to_planes(resp_real.reshape(flat_shape), resp_imag.reshape(flat_shape))
    grid_shape = (own_count, half_len, local_first, local_second)
    resp_real = resp_real.reshape(grid_shape)
    resp_imag = resp_imag.reshape(grid_shape)
    force_field = jnp.einsum("vkxy,kz->vxyz", resp_real, cos_back, precision=highest) - jnp.einsum(
        "vkxy,kz->vxyz", resp_imag, sin_back, precision=highest
    )
    chemical = (
        order_field
        - landau_cubic * order_field * order_field
        + landau_quartic * order_field * total_sq[None]
    )
    return order_field - mobility * (chemical + force_field)


def solution(mesh):
    placed = (P("var", "py", "pz", None), P(), P())
    return jax.shard_map(
        shards, mesh=mesh, in_specs=placed, out_specs=P("var", "py", "pz", None), check_vma=False
    )
```

profile of v0, /device:TPU:1, one launch (start us, length us, event | category | flops | bytes accessed | tf_op | source)
XLA Modules:
  0.0 723.1 jit_solution(15371404697599237691)
XLA Ops:
  19.3 12.5 %all-to-all-start.1 = ((f32[6,128,1024]{2,0,1:T(8,128)}), f32[6,128,1024]{2,0,1:T(8,128)}, u32[]{:S(2)}, u32[]{:S(2)}) async-start(f32[6,128,1024]{2,0,1:T(8,128)} %copy.41), calls=%async_computation.1 | async-start | bytes 8388608 | tf_op jit(solution)/shard_map/all_to_all | solution.py:134
  44.8 40.4 %all-to-all-done.1 = f32[6,128,1024]{2,0,1:T(8,128)} async-done(((f32[6,128,1024]{2,0,1:T(8,128)}), f32[6,128,1024]{2,0,1:T(8,128)}, u32[]{:S(2)}, u32[]{:S(2)}) %all-to-all-start.1) | async-done | bytes 3145760 | tf_op jit(solution)/shard_map/all_to_all | solution.py:134
  109.3 13.8 %fusion.2 = f32[6,8,2,32,256,1]{4,3,5,2,1,0:T(8,128)} fusion(f32[6,8,8,2,32,32]{5,4,0,3,2,1:T(8,128)} %reshape.347, s32[8,32]{1,0:T(8,128)S(1)} %multiply_add_fusion.5), kind=kOutput, calls=%fused_computation.4 | convolution fusion | flops 2416836608 | bytes 6292480 | tf_op jit(solution)/shard_map/vacqxy,cyn->vaqxn/dot_general | solution.py:96
  123.0 10.4 %fusion = f32[6,8,2,32,256,1]{4,3,5,2,1,0:T(8,128)S(1)} fusion(f32[6,8,8,2,32,32]{5,4,0,3,2,1:T(8,128)S(1)} %copy-done.3, s32[8,32]{1,0:T(8,128)S(1)} %multiply_add_fusion.5), kind=kOutput, calls=%fused_computation.2 | convolution fusion | flops 2416836608 | bytes 6292480 | tf_op jit(solution)/shard_map/vacqxy,cyn->vaqxn/dot_general | solution.py:95
  133.5 12.5 %all-to-all-done = f32[6,128,1024]{2,0,1:T(8,128)} async-done(((f32[6,128,1024]{2,0,1:T(8,128)}), f32[6,128,1024]{2,0,1:T(8,128)}, u32[]{:S(2)}, u32[]{:S(2)}) %all-to-all-start) | async-done | bytes 3145760 | tf_op jit(solution)/shard_map/all_to_all | solution.py:133
  155.6 13.8 %fusion.35 = f32[6,8,2,32,256]{4,3,2,1,0:T(8,128)S(1)} fusion(f32[6,8,2,32,256,1]{4,3,5,2,1,0:T(8,128)} %fusion.2, f32[6,8,8,2,32,32]{5,4,0,3,2,1:T(8,128)} %reshape.346, s32[8,32]{1,0:T(8,128)S(1)} %multiply_add_fusion.5), kind=kOutput, calls=%fused_computation.43 | convolution fusion | flops 2418409472 | bytes 9438208 | tf_op jit(solution)/shard_map/vacqxy,cyn->vaqxn/dot_general | solution.py:93
  173.3 10.5 %fusion.34 = f32[6,8,2,32,256]{4,3,2,1,0:T(8,128)S(1)} fusion(f32[6,8,2,32,256,1]{4,3,5,2,1,0:T(8,128)S(1)} %fusion, f32[6,8,8,2,32,32]{5,4,0,3,2,1:T(8,128)S(1)} %copy-done.2, s32[8,32]{1,0:T(8,128)S(1)} %multiply_add_fusion.5), kind=kOutput, calls=%fused_computation.41 | convolution fusion | flops 2418409472 | bytes 9438208 | tf_op jit(solution)/shard_map/vacqxy,cyn->vaqxn/dot_general | solution.py:94
  192.0 10.5 %multiply_reduce_fusion.4 = (f32[2,256,256]{2,1,0:T(8,128)S(1)}, f32[2,256,256]{2,1,0:T(8,128)S(1)}, f32[2,256,256]{2,1,0:T(8,128)S(1)}, f32[2,256,256]{2,1,0:T(...) fusion(f32[2,256,256]{2,1,0:T(8,128)S(1)} %copy-done.9, ...), kind=kOutput, calls=%fused_computation.50 | convolution fusion | flops 2445672448 | bytes 18351320 | tf_op jit(solution)/shard_map/vaqxn,axm->vqmn/dot_general | solution.py:94
  205.8 11.0 %fusion.12 = f32[12,2,256,256]{3,0,2,1:T(8,128)S(1)} fusion(f32[6,2,256,256]{3,2,1,0:T(8,128)} %get-tuple-element.54, f32[12,12]{0,1:T(8,128)S(1)} %convolution_bitcast_fusion, s32[]{:T(128)S(6)} %select_n.139), kind=kOutput, calls=%fused_computation.16 | convolution fusion | flops 113246208 | bytes 9441284 | tf_op jit(solution)/shard_map/pq,qabc->pabc/dot_general | solution.py:88
  239.5 102.3 %all-reduce.3.cloned.1.call-done = (f32[4,2,256,256]{3,2,1,0:T(8,128)}, f32[4,2,256,256]{3,2,1,0:T(8,128)}, f32[32,32,256]{2,1,0:T(8,128)}) async-done(((f32[4,2,256,256]{3,2,1,0:T(8,128)}, f32[4,2,256,256]{3,2,1,0:T(8,128)}, f32[32,32,256]{2,1,0:T(8,128)}), (f32[4,2,256,256]{3,2,1,0:T(8,128)}, f32[4,2,256,256]{3,2,1,0:T(8,128)}, f32[32,32,256]{2,1,0:T(8,128)})) %all-reduce.3.cloned.1.call-update) | async-done | bytes 5242896 | tf_op jit(solution)/shard_map/psum | solution.py:175
  346.3 78.7 %reduce-scatter.5.cloned.1.call-done = f32[6,2,256,256]{3,2,1,0:T(8,128)} async-done(((f32[12,2,256,256]{3,2,1,0:T(8,128)}), f32[6,2,256,256]{3,2,1,0:T(8,128)}) %reduce-scatter.5.cloned.1.call-update) | async-done | bytes 3145744 | tf_op jit(solution)/shard_map/reduce_scatter | solution.py:173
  442.2 65.9 %reduce-scatter.3.cloned.1.call-done = f32[6,2,256,256]{3,2,1,0:T(8,128)} async-done(((f32[12,2,256,256]{3,2,1,0:T(8,128)}), f32[6,2,256,256]{3,2,1,0:T(8,128)}) %reduce-scatter.3.cloned.1.call-update) | async-done | bytes 3145744 | tf_op jit(solution)/shard_map/reduce_scatter | solution.py:172
  522.5 11.9 %fusion.24 = f32[8,32,6,8,2,32]{5,1,4,3,2,0:T(8,128)S(1)} fusion(f32[6,8,2,32,256]{4,3,2,0,1:T(8,128)S(1)} %subtract_bitcast_fusion.1, s32[8,32]{1,0:T(8,128)S(1)} %multiply_add_fusion.5), kind=kOutput, calls=%fused_computation.30 | convolution fusion | flops 2416836608 | bytes 6292480 | tf_op jit(solution)/shard_map/vaqxn,ncy->vacqxy/dot_general | solution.py:93
  534.4 15.9 %subtract_bitcast_fusion = f32[6,8,8,2,32,32]{4,5,3,1,0,2:T(8,128)} fusion(f32[8,32,6,8,2,32]{5,1,4,3,2,0:T(8,128)S(1)} %fusion.24, f32[6,8,2,32,256]{4,3,2,0,1:T(8,128)S(1)} %add_bitcast_fusion.1, s32[8,32]{1,0:T(8,128)S(1)} %multiply_add_fusion.5), kind=kOutput, calls=%fused_computation.1 | convolution fusion | flops 2417623040 | bytes 9438208 | tf_op jit(solution)/shard_map/vaqxn,ncy->vacqxy/dot_general | solution.py:96
  550.3 12.6 %copy.85 = f32[6,8,8,2,32,32]{5,4,0,3,2,1:T(8,128)} copy(f32[6,8,8,2,32,32]{4,5,3,1,0,2:T(8,128)} %subtract_bitcast_fusion) | data formatting | bytes 6291456 | tf_op jit(solution)/shard_map/reshape | solution.py:199
  562.9 10.9 %reshape.344 = f32[6,128,1024]{2,0,1:T(8,128)} reshape(f32[6,8,8,2,32,32]{5,4,0,3,2,1:T(8,128)} %copy.85) | data formatting | bytes 6291456 | tf_op jit(solution)/shard_map/reshape | solution.py:199
  573.8 10.4 %all-to-all-start.2 = ((f32[6,128,1024]{2,0,1:T(8,128)}), f32[6,128,1024]{2,0,1:T(8,128)}, u32[]{:S(2)}, u32[]{:S(2)}) async-start(f32[6,128,1024]{2,0,1:T(8,128)} %reshape.344), calls=%async_computation.4 | async-start | bytes 8388608 | tf_op jit(solution)/shard_map/all_to_all | solution.py:133
  584.2 13.4 %fusion.20 = f32[8,32,6,8,2,32]{5,1,4,3,2,0:T(8,128)S(1)} fusion(f32[6,8,2,32,256]{4,3,2,0,1:T(8,128)} %copy-done.4, s32[8,32]{1,0:T(8,128)S(1)} %multiply_add_fusion.5), kind=kOutput, calls=%fused_computation.26 | convolution fusion | flops 2416836608 | bytes 6292480 | tf_op jit(solution)/shard_map/vaqxn,ncy->vacqxy/dot_general | solution.py:95
  597.6 16.2 %add_bitcast_fusion = f32[6,8,8,2,32,32]{4,5,3,1,0,2:T(8,128)} fusion(f32[8,32,6,8,2,32]{5,1,4,3,2,0:T(8,128)S(1)} %fusion.20, f32[6,8,2,32,256]{4,3,2,0,1:T(8,128)S(1)} %subtract_bitcast_fusion.1, s32[8,32]{1,0:T(8,128)S(1)} %multiply_add_fusion.5), kind=kOutput, calls=%fused_computation | convolution fusion | flops 2417623040 | bytes 9438208 | tf_op jit(solution)/shard_map/vaqxn,ncy->vacqxy/dot_general | solution.py:94
  613.8 12.6 %copy.86 = f32[6,8,8,2,32,32]{5,4,0,3,2,1:T(8,128)} copy(f32[6,8,8,2,32,32]{4,5,3,1,0,2:T(8,128)} %add_bitcast_fusion) | data formatting | bytes 6291456 | tf_op jit(solution)/shard_map/reshape | solution.py:199
  626.5 10.7 %reshape.345 = f32[6,128,1024]{2,0,1:T(8,128)} reshape(f32[6,8,8,2,32,32]{5,4,0,3,2,1:T(8,128)} %copy.86) | data formatting | bytes 6291456 | tf_op jit(solution)/shard_map/reshape | solution.py:199
  637.6 10.6 %all-to-all-start.3 = ((f32[6,128,1024]{2,0,1:T(8,128)}), f32[6,128,1024]{2,0,1:T(8,128)}, u32[]{:S(2)}, u32[]{:S(2)}) async-start(f32[6,128,1024]{2,0,1:T(8,128)} %reshape.345), calls=%async_computation.5 | async-start | bytes 8388608 | tf_op jit(solution)/shard_map/all_to_all | solution.py:134
  660.0 41.5 %all-to-all-done.3 = f32[6,128,1024]{2,0,1:T(8,128)} async-done(((f32[6,128,1024]{2,0,1:T(8,128)}), f32[6,128,1024]{2,0,1:T(8,128)}, u32[]{:S(2)}, u32[]{:S(2)}) %all-to-all-start.3) | async-done | bytes 3145760 | tf_op jit(solution)/shard_map/all_to_all | solution.py:134
  705.2 10.9 %fusion.11 = f32[6,32,32,256]{3,2,1,0:T(8,128)} fusion(f32[6,32,32,256]{3,2,1,0:T(8,128)} %param.3, f32[6,32,32,256]{3,2,1,0:T(8,128)} %fusion.100, f32[32,32,256]{2,1,0:T(8,128)} %broadcast_multiply_fusion, f32[6,128,32,32]{1,3,2,0:T(8,128)S(1)} %bitcast.259, f32[256,256]{1,0:T(8,128)S(1)} %copy-done.12, f32[128]{0:T(128)S(1)} %compare_select_fusion.1), kind=kOutput, calls=%fused_computation.14 | convolution fusion | flops 2430107648 | bytes 23200256 | tf_op jit(solution)/shard_map/vkxy,kz->vxyz/dot_general | solution.py:203
  (87 shorter events, 149.0 us)
Async XLA Ops:
  6.5 38.1 %copy-start = (f32[24,6]{0,1:T(8,128)S(1)}, f32[24,6]{0,1:T(8,128)}, u32[]{:S(2)}) copy-start(f32[24,6]{0,1:T(8,128)} %param.4) | copy-start | bytes 1732
  7.5 8.4 %copy-start.11 = (f32[256,256]{1,0:T(8,128)}, f32[256,256]{1,0:T(8,128)S(1)}, u32[]{:S(2)}) copy-start(f32[256,256]{1,0:T(8,128)S(1)} %fusion.109) | copy-start | bytes 786436
  19.3 65.9 %all-to-all-start.1 = ((f32[6,128,1024]{2,0,1:T(8,128)}), f32[6,128,1024]{2,0,1:T(8,128)}, u32[]{:S(2)}, u32[]{:S(2)}) async-start(f32[6,128,1024]{2,0,1:T(8,128)} %copy.41), calls=%async_computation.1 | async-start | bytes 8388608 | tf_op jit(solution)/shard_map/all_to_all | solution.py:134
  32.8 8.3 %copy-start.13 = (f32[256,256]{1,0:T(8,128)}, f32[256,256]{1,0:T(8,128)S(1)}, u32[]{:S(2)}) copy-start(f32[256,256]{1,0:T(8,128)S(1)} %fusion.110) | copy-start | bytes 786436
  41.1 3.5 copy-start.16
  85.2 60.8 %all-to-all-start = ((f32[6,128,1024]{2,0,1:T(8,128)}), f32[6,128,1024]{2,0,1:T(8,128)}, u32[]{:S(2)}, u32[]{:S(2)}) async-start(f32[6,128,1024]{2,0,1:T(8,128)} %copy.38), calls=%async_computation | async-start | bytes 8388608 | tf_op jit(solution)/shard_map/all_to_all | solution.py:133
  92.6 249.3 %all-reduce.3.cloned.1.call-start = ((), (), s32[]{:S(2)}) async-start(), calls=%async_computation.8 | async-start | bytes 10485760 | tf_op jit(solution)/shard_map/psum | solution.py:175
  109.3 13.8 %copy-start.3 = (f32[6,8,8,2,32,32]{5,4,0,3,2,1:T(8,128)S(1)}, f32[6,8,8,2,32,32]{5,4,0,3,2,1:T(8,128)}, u32[]{:S(2)}) copy-start(f32[6,8,8,2,32,32]{5,4,0,3,2,1:T(8,128)} %reshape.347) | copy-start | bytes 9437188
  155.6 17.7 %copy-start.2 = (f32[6,8,8,2,32,32]{5,4,0,3,2,1:T(8,128)S(1)}, f32[6,8,8,2,32,32]{5,4,0,3,2,1:T(8,128)}, u32[]{:S(2)}) copy-start(f32[6,8,8,2,32,32]{5,4,0,3,2,1:T(8,128)} %reshape.346) | copy-start | bytes 9437188
  187.7 4.3 copy-start.7
  187.7 4.3 copy-start.8
  187.7 4.3 copy-start.9
  205.6 219.5 %reduce-scatter.5.cloned.1.call-start = ((), (), s32[]{:S(2)}) async-start(), calls=%async_computation.7 | async-start | bytes 9437184 | tf_op jit(solution)/shard_map/reduce_scatter | solution.py:173
  223.4 284.7 %reduce-scatter.3.cloned.1.call-start = ((), (), s32[]{:S(2)}) async-start(), calls=%async_computation.6 | async-start | bytes 9437184 | tf_op jit(solution)/shard_map/reduce_scatter | solution.py:172
  341.8 3.1 copy-start.10
  508.1 6.1 copy-start.6
  514.2 4.2 copy-start.5
  518.4 16.0 %copy-start.4 = (f32[6,8,2,32,256]{4,3,2,0,1:T(8,128)}, f32[6,8,2,32,256]{4,3,2,0,1:T(8,128)S(1)}, u32[]{:S(2)}) copy-start(f32[6,8,2,32,256]{4,3,2,0,1:T(8,128)S(1)} %add_bitcast_fusion.1) | copy-start | bytes 9437188
  573.8 63.8 %all-to-all-start.2 = ((f32[6,128,1024]{2,0,1:T(8,128)}), f32[6,128,1024]{2,0,1:T(8,128)}, u32[]{:S(2)}, u32[]{:S(2)}) async-start(f32[6,128,1024]{2,0,1:T(8,128)} %reshape.344), calls=%async_computation.4 | async-start | bytes 8388608 | tf_op jit(solution)/shard_map/all_to_all | solution.py:133
  637.2 11.1 %copy-start.15 = (f32[32,32,256]{2,1,0:T(8,128)S(1)}, f32[32,32,256]{2,1,0:T(8,128)}, u32[]{:S(2)}) copy-start(f32[32,32,256]{2,1,0:T(8,128)} %get-tuple-element.19) | copy-start | bytes 3145732
  637.6 63.9 %all-to-all-start.3 = ((f32[6,128,1024]{2,0,1:T(8,128)}), f32[6,128,1024]{2,0,1:T(8,128)}, u32[]{:S(2)}, u32[]{:S(2)}) async-start(f32[6,128,1024]{2,0,1:T(8,128)} %reshape.345), calls=%async_computation.5 | async-start | bytes 8388608 | tf_op jit(solution)/shard_map/all_to_all | solution.py:134
  649.4 3.7 copy-start.14
  660.0 45.1 %copy-start.12 = (f32[256,256]{1,0:T(8,128)S(1)}, f32[256,256]{1,0:T(8,128)}, u32[]{:S(2)}) copy-start(f32[256,256]{1,0:T(8,128)} %copy-done.11) | copy-start | bytes 786436
  705.2 11.0 %copy-start.1 = (f32[24,6]{0,1:T(8,128)S(1)}, f32[24,6]{0,1:T(8,128)}, u32[]{:S(2)}) copy-start(f32[24,6]{0,1:T(8,128)} %param.4) | copy-start | bytes 1732
Sparse Core Ops, SparseCore 0:
  205.7 136.0 all-reduce.2
  344.4 80.6 reduce-scatter.4
  427.5 80.5 reduce-scatter.2
where the time goes:
time: 733 us; the launch traced here: 723 us
  waiting for transfers between devices  342 us (47%)
  matrix products  203 us (28%)
  local copies, waits for them, and re-layouts  93.5 us (13%)
  starting transfers between devices  41.2 us (6%)
  other arithmetic  29.5 us (4%)
  between operations  14 us (2%)
    psum x1, waiting for transfers between devices, shards(): shared_real, shared_imag = lax.psum((shared_real, shared_imag), 'var')  102 us
    all_to_all x2, waiting for transfers between devices, to_planes(): lax.all_to_all(second_part, ('py', 'pz'), split_axis=1, concat_axis=1, ti...  81.9 us
    reduce_scatter x1, waiting for transfers between devices, shards(): lax.psum_scatter(mix_imag, 'var', scatter_dimension=0, tiled=True)  78.7 us
    reduce_scatter x1, waiting for transfers between devices, shards(): lax.psum_scatter(mix_real, 'var', scatter_dimension=0, tiled=True)  65.9 us
    dot_general x4, matrix products, complex_section(): real_sin = jnp.einsum(pattern, real_part, sin_table, precision=highest)  41.3 us
    dot_general x4, matrix products, complex_section(): imag_sin = jnp.einsum(pattern, imag_part, sin_table, precision=highest)  39.4 us
    dot_general x4, matrix products, complex_section(): real_cos = jnp.einsum(pattern, real_part, cos_table, precision=highest)  33.6 us
    dot_general x4, matrix products, complex_section(): imag_cos = jnp.einsum(pattern, imag_part, cos_table, precision=highest)  33.2 us
  transfers between devices with their start and end apart: 7, of which 7 were waited for; matrix products, arithmetic and copies ran while one was open for 24% of the time, Pallas kernels for 0%

commit v1 on v0

v1 whole, which is shorter than its diff:
```python
import functools

import jax
import jax.numpy as jnp
import ml_dtypes
import numpy as np
from jax import lax
from jax.experimental import pallas as pl
from jax.experimental.pallas import tpu as pltpu
from jax.sharding import PartitionSpec as P

lame_first = 1.5
shear_mod = 1.0
relax_coef = 1.0 / 1.4
grad_coef = 0.5
mobility = 0.2
landau_cubic = 3.0
landau_quartic = 0.5
two_pi = 6.283185307179586
highest = lax.Precision.HIGHEST
every = ("var", "py", "pz")
vmem_bytes = 48 * 1024 * 1024

forward_chunks = ((0, 1), (2,))
backward_chunks = ((0,), (1, 2))


def split_table(table):
    high = table.astype(ml_dtypes.bfloat16)
    low = (table - high.astype(np.float64)).astype(ml_dtypes.bfloat16)
    return high, low


def left_table(table):
    high, low = split_table(table)
    return np.concatenate([high, low, high], axis=1)


def right_table(table):
    high, low = split_table(table)
    return np.concatenate([high, high, low], axis=0)


@functools.cache
def dft_tables(length):
    half = length // 2
    ids = np.arange(length)
    angles = (ids[:, None] * ids[None, :] % length) * (2.0 * np.pi / length)
    cos, sin = np.cos(angles), np.sin(angles)
    z_fwd = left_table(np.concatenate([cos[:half], -sin[:half]], axis=0))
    weight = np.where(np.arange(half) == 0, 1.0, 2.0)[:, None]
    z_back = right_table(np.concatenate([cos[:half] * weight, -sin[:half] * weight], axis=0))
    y_both = left_table(np.concatenate([cos, sin], axis=0))
    blocks = 8
    width = length // blocks
    fwd = np.empty((2, length, 2, length))
    fwd[0, :, 0], fwd[0, :, 1] = cos, -sin
    fwd[1, :, 0], fwd[1, :, 1] = sin, cos
    fwd = fwd.reshape(2, blocks // 2, 2, width, 2 * length).transpose(1, 0, 2, 3, 4)
    x_fwd = right_table(fwd.reshape(2 * length, 2 * length))
    back = np.empty((2, length, 2, length))
    back[0, :, 0], back[0, :, 1] = cos, sin
    back[1, :, 0], back[1, :, 1] = -sin, cos
    back = back.reshape(2 * length, 2, blocks // 2, 2, width).transpose(0, 2, 1, 3, 4)
    x_back = right_table(back.reshape(2 * length, 2 * length))
    return z_fwd, z_back, y_both, x_fwd, x_back


def split_value(value):
    high = value.astype(jnp.bfloat16)
    low = (value - high.astype(jnp.float32)).astype(jnp.bfloat16)
    return high, low


def as_left(value):
    high, low = split_value(value)
    return jnp.concatenate([high, low, high], axis=1)


def as_right(value):
    high, low = split_value(value)
    return jnp.concatenate([high, high, low], axis=0)


def matmul(left, right):
    return lax.dot_general(
        left, right, (((1,), (0,)), ((), ())), preferred_element_type=jnp.float32
    )


def matmul_tr(left, right):
    return lax.dot_general(
        left, right, (((1,), (1,)), ((), ())), preferred_element_type=jnp.float32
    )


def lane_ids(rows):
    return lax.broadcasted_iota(jnp.int32, (rows, 128), 1)


def z_forward(first_ref, second_ref, table_ref, *refs):
    out_ref, sq_ref = refs[-2:]
    group = pl.program_id(1)
    for side, ref in enumerate((first_ref, second_ref)):
        phi = ref[...]
        squares = phi[0] * phi[0] + phi[1] * phi[1]
        lanes = slice(side * 128, side * 128 + 128)
        before = refs[0][:, :, lanes] if len(refs) == 3 else 0.0
        sq_ref[:, :, lanes] = jnp.where(group > 0, sq_ref[:, :, lanes], before) + squares

    row_refs = [first_ref.reshape(512, 128), second_ref.reshape(512, 128)]
    flat_ref = out_ref.reshape(1024, 128)
    low_half = lane_ids(128) < 64
    for batch in range(2):
        block = jnp.concatenate(
            [
                jnp.concatenate(
                    [ref[pl.ds(batch * 4 + y, 64, stride=8), :] for ref in row_refs], axis=1
                )
                for y in range(4)
            ],
            axis=0,
        )
        high, low = split_value(block)
        spectrum = matmul_tr(table_ref[...], jnp.concatenate([high, high, low], axis=1))
        for pair in range(2):
            real = spectrum[:128, pair * 128 : pair * 128 + 128]
            imag = spectrum[128:, pair * 128 : pair * 128 + 128]
            even = jnp.where(low_half, real, pltpu.roll(imag, 64, 1))
            odd = jnp.where(low_half, pltpu.roll(real, 64, 1), imag)
            y = batch * 4 + pair * 2
            flat_ref[pl.ds(y, 128, stride=8), :] = even
            flat_ref[pl.ds(y + 1, 128, stride=8), :] = odd


def xy_forward(in_ref, y_ref, x_ref, out_ref, left_ref):
    lanes = lane_ids(256)
    low_half = lanes < 64
    even_lane = (lanes // 32) % 2 == 0
    for pair in range(4):
        first = in_ref[pair * 16 : pair * 16 + 8].reshape(256, 128)
        second = in_ref[pair * 16 + 8 : pair * 16 + 16].reshape(256, 128)
        both = matmul(y_ref[...], as_right(jnp.concatenate([first, second], axis=1)))
        done = []
        for side in range(2):
            cos_part = both[:256, side * 128 : side * 128 + 128]
            sin_part = pltpu.roll(both[256:, side * 128 : side * 128 + 128], 64, 1)
            done.append(cos_part + jnp.where(low_half, sin_part, -sin_part))
        zero = jnp.where(even_lane, done[0], pltpu.roll(done[1], 32, 1))
        one = jnp.where(even_lane, pltpu.roll(done[0], 96, 1), done[1])
        for v, value in enumerate((zero, one)):
            high, low = split_value(value)
            rows = slice(v * 256, v * 256 + 256)
            left_ref[rows, pair * 128 : pair * 128 + 128] = high
            left_ref[rows, 512 + pair * 128 : 512 + pair * 128 + 128] = low
            left_ref[rows, 1024 + pair * 128 : 1024 + pair * 128 + 128] = high
    for v in range(2):
        out_ref[v] = matmul(left_ref[v * 256 : v * 256 + 256, :], x_ref[...])


def xy_back(in_ref, x_ref, y_ref, out_ref, mid_ref):
    lanes = lane_ids(256)
    low_half = lanes < 64
    even_lane = (lanes // 32) % 2 == 0
    for v in range(2):
        mid_ref[v] = matmul(as_left(in_ref[v]), x_ref[...])
    for pair in range(4):
        zero = mid_ref[0, :, pair * 128 : pair * 128 + 128]
        one = mid_ref[1, :, pair * 128 : pair * 128 + 128]
        first = jnp.where(even_lane, zero, pltpu.roll(one, 32, 1))
        second = jnp.where(even_lane, pltpu.roll(zero, 96, 1), one)
        both = matmul(y_ref[...], as_right(jnp.concatenate([first, second], axis=1)))
        for side in range(2):
            cos_part = both[:256, side * 128 : side * 128 + 128]
            sin_part = pltpu.roll(both[256:, side * 128 : side * 128 + 128], 64, 1)
            value = cos_part + jnp.where(low_half, -sin_part, sin_part)
            start = pair * 16 + side * 8
            out_ref[start : start + 8] = value.reshape(8, 32, 128)


def mix_kernel(n_in, n_out, places_in, places_out, rows, length, coef_ref, *refs):
    ins, outs = refs[:n_in], refs[n_in : n_in + n_out]
    half = length // 2
    wave_z = coef_ref[12, 0]
    base = pl.program_id(0) * rows
    volume = 1.0 / float(length * length * length)

    def tile(index, carry):
        row = pl.multiple_of(index * 8, 8)
        ky = lax.broadcasted_iota(jnp.int32, (8, length), 0) + (base + row)
        kx = lax.broadcasted_iota(jnp.int32, (8, length), 1)
        wy = jnp.where(ky >= half, ky - length, ky).astype(jnp.float32)
        wx = jnp.where(kx >= half, kx - length, kx).astype(jnp.float32)
        wz = jnp.full((8, length), wave_z, jnp.float32)
        squared = wx * wx + wy * wy + wz * wz
        inverse = 1.0 / jnp.maximum(squared, 1.0)
        keep = jnp.where((ky == half) | (kx == half), 0.0, volume)
        grad = keep * squared * (grad_coef * (two_pi / length) ** 2)

        def field(p):
            place, group, var, v = places_in[p]
            return ins[place][group, var, v, pl.ds(row, 8), :]

        strains = []
        for q in range(12):
            value = field(q)
            for m in range(6):
                term = coef_ref[q, m] * value
                if q == 0:
                    strains.append(term)
                else:
                    strains[m] = strains[m] + term
        drives = []
        for part in range(2):
            strain = [total[:, part * length : (part + 1) * length] for total in strains]
            trace = lame_first * (strain[0] + strain[1] + strain[2])
            s11 = trace + 2.0 * shear_mod * strain[0]
            s22 = trace + 2.0 * shear_mod * strain[1]
            s33 = trace + 2.0 * shear_mod * strain[2]
            s23 = 2.0 * shear_mod * strain[3]
            s13 = 2.0 * shear_mod * strain[4]
            s12 = 2.0 * shear_mod * strain[5]
            t1 = (s11 * wx + s12 * wy + s13 * wz) * inverse
            t2 = (s12 * wx + s22 * wy + s23 * wz) * inverse
            t3 = (s13 * wx + s23 * wy + s33 * wz) * inverse
            normal = (wx * t1 + wy * t2 + wz * t3) * (relax_coef * inverse)
            u1 = t1 - normal * wx
            u2 = t2 - normal * wy
            u3 = t3 - normal * wz
            drives.append(
                [
                    keep * (strain[0] - wx * u1),
                    keep * (strain[1] - wy * u2),
                    keep * (strain[2] - wz * u3),
                    keep * (2.0 * strain[3] - (wy * u3 + wz * u2)),
                    keep * (2.0 * strain[4] - (wx * u3 + wz * u1)),
                    keep * (2.0 * strain[5] - (wx * u2 + wy * u1)),
                ]
            )
        drive = [jnp.concatenate([drives[0][m], drives[1][m]], axis=1) for m in range(6)]
        both_grad = jnp.concatenate([grad, grad], axis=1)
        for p in range(12):
            total = both_grad * field(p)
            for m in range(6):
                total = total + coef_ref[p, 6 + m] * drive[m]
            place, group, var, v = places_out[p]
            outs[place][group, var, v, pl.ds(row, 8), :] = total
        return carry

    lax.fori_loop(0, rows // 8, tile, 0)


def z_back(spec_ref, phi_ref, own_ref, partner_ref, table_ref, *rest):
    out_ref, force_ref = rest[-2:]
    flat_ref = spec_ref.reshape(1024, 128)
    row_refs = [force_ref.at[side].reshape(512, 128) for side in range(2)]
    for batch in range(2):
        lefts = []
        for y in range(4):
            turned = flat_ref[pl.ds(batch * 4 + y, 128, stride=8), :].T
            lefts.append(jnp.concatenate([turned[:64], turned[64:]], axis=1))
        force = matmul(as_left(jnp.concatenate(lefts, axis=0)), table_ref[...])
        for y in range(4):
            rows = pl.ds(batch * 4 + y, 64, stride=8)
            for side, ref in enumerate(row_refs):
                lanes = slice(side * 128, side * 128 + 128)
                ref[rows, :] = force[y * 64 : y * 64 + 64, lanes]
    for side in range(2):
        lanes = slice(side * 128, side * 128 + 128)
        total_sq = own_ref[:, :, lanes] + partner_ref[:, :, lanes]
        for v in range(2):
            phi = phi_ref[v, :, :, lanes]
            chemical = phi - landau_cubic * phi * phi + landau_quartic * phi * total_sq
            out_ref[v, :, :, lanes] = phi - mobility * (chemical + force_ref[side, v])


def params(count):
    return pltpu.CompilerParams(
        dimension_semantics=("arbitrary",) * count, vmem_limit_bytes=vmem_bytes
    )


def cost(flops, moved):
    return pl.CostEstimate(flops=int(flops), bytes_accessed=int(moved), transcendentals=0)


def whole(array):
    return pl.BlockSpec(array.shape, lambda *ids: (0,) * array.ndim)


group_bytes = 2 * 32 * 32 * 256 * 4


def call_z_forward(phi, table, chunk, squares):
    count, start = len(chunk), chunk[0]
    earlier = [] if squares is None else [squares]
    return pl.pallas_call(
        z_forward,
        grid=(4, count),
        in_specs=[
            pl.BlockSpec((2, 32, 8, 128), lambda j, g: (g + start, 0, j, 0)),
            pl.BlockSpec((2, 32, 8, 128), lambda j, g: (g + start, 0, j, 1)),
            whole(table),
        ]
        + [pl.BlockSpec((32, 8, 256), lambda j, g: (0, j, 0)) for _ in earlier],
        out_specs=[
            pl.BlockSpec((128, 8, 128), lambda j, g: (0, g * 4 + j, 0)),
            pl.BlockSpec((32, 8, 256), lambda j, g: (0, j, 0)),
        ],
        out_shape=[
            jax.ShapeDtypeStruct((128, 32 * count, 128), jnp.float32),
            jax.ShapeDtypeStruct((32, 32, 256), jnp.float32),
        ],
        compiler_params=params(2),
        cost_estimate=cost(count * 0.81e9, count * 2 * group_bytes),
        name="z_forward",
    )(phi, phi, table, *earlier)


def call_xy_forward(spec, y_table, x_table, chunk):
    count = len(chunk)
    return pl.pallas_call(
        xy_forward,
        grid=(count, 2),
        in_specs=[
            pl.BlockSpec((64, 32, 128), lambda g, a: (a, g, 0)),
            whole(y_table),
            whole(x_table),
        ],
        out_specs=pl.BlockSpec((None, None, 2, 256, 512), lambda g, a: (g, a, 0, 0, 0)),
        out_shape=jax.ShapeDtypeStruct((count, 2, 2, 256, 512), jnp.float32),
        scratch_shapes=[pltpu.VMEM((512, 1536), jnp.bfloat16)],
        compiler_params=params(2),
        cost_estimate=cost(count * 3.2e9, count * 2 * group_bytes),
        name="xy_forward",
    )(spec, y_table, x_table)


def call_mix(coefs, specs, length):
    rows = 32

    def places(chunks):
        where = {g: (c, i) for c, chunk in enumerate(chunks) for i, g in enumerate(chunk)}
        return tuple(where[p % 6 // 2] + (p // 6, p % 2) for p in range(12))

    def spec_of(chunk):
        return pl.BlockSpec((len(chunk), 2, 2, rows, 512), lambda j: (0, 0, 0, j, 0))

    body = functools.partial(
        mix_kernel,
        len(forward_chunks),
        len(backward_chunks),
        places(forward_chunks),
        places(backward_chunks),
        rows,
        length,
    )
    return pl.pallas_call(
        body,
        grid=(length // rows,),
        in_specs=[pl.BlockSpec(memory_space=pltpu.SMEM)] + [spec_of(c) for c in forward_chunks],
        out_specs=[spec_of(c) for c in backward_chunks],
        out_shape=[
            jax.ShapeDtypeStruct((len(c), 2, 2, 256, 512), jnp.float32) for c in backward_chunks
        ],
        compiler_params=params(1),
        cost_estimate=cost(50e6, 6 * group_bytes),
        name="mixing",
    )(coefs, *specs)


def call_xy_back(resp, x_table, y_table, chunk):
    count = len(chunk)
    return pl.pallas_call(
        xy_back,
        grid=(count, 2),
        in_specs=[
            pl.BlockSpec((None, None, 2, 256, 512), lambda g, a: (g, a, 0, 0, 0)),
            whole(x_table),
            whole(y_table),
        ],
        out_specs=pl.BlockSpec((64, 32, 128), lambda g, a: (a, g, 0)),
        out_shape=jax.ShapeDtypeStruct((128, 32 * count, 128), jnp.float32),
        scratch_shapes=[pltpu.VMEM((2, 256, 512), jnp.float32)],
        compiler_params=params(2),
        cost_estimate=cost(count * 3.2e9, count * 2 * group_bytes),
        name="xy_back",
    )(resp, x_table, y_table)


def call_z_back(spec, phi, own, partner, table, chunk, partial):
    count, start = len(chunk), chunk[0]
    operands = [spec, phi, own, partner, table]
    specs = [
        pl.BlockSpec((128, 8, 128), lambda j, g: (0, g * 4 + j, 0)),
        pl.BlockSpec((2, 32, 8, 256), lambda j, g: (g + start, 0, j, 0)),
        pl.BlockSpec((32, 8, 256), lambda j, g: (0, j, 0)),
        pl.BlockSpec((32, 8, 256), lambda j, g: (0, j, 0)),
        whole(table),
    ]
    aliases = {}
    if partial is not None:
        operands.append(partial)
        specs.append(pl.BlockSpec(memory_space=pl.ANY))
        aliases = {5: 0}
    return pl.pallas_call(
        z_back,
        grid=(4, count),
        in_specs=specs,
        out_specs=pl.BlockSpec((2, 32, 8, 256), lambda j, g: (g + start, 0, j, 0)),
        out_shape=jax.ShapeDtypeStruct(phi.shape, jnp.float32),
        input_output_aliases=aliases,
        scratch_shapes=[pltpu.VMEM((2, 2, 32, 8, 128), jnp.float32)],
        compiler_params=params(2),
        cost_estimate=cost(count * 0.81e9, count * 3 * group_bytes),
        name="z_back",
    )(*operands)


def exchange(block):
    return lax.all_to_all(block, every, split_axis=0, concat_axis=0, tiled=True)


def after(block, earlier):
    return lax.optimization_barrier((block, earlier[-1]))[0] if earlier else block


def coefficients(strains, variant_strain, variants):
    bank_rows = strains.shape[0]
    picked = variant_strain[:variants]
    one_hot = (picked[:, None] == jnp.arange(bank_rows, dtype=jnp.int32)[None, :]).astype(
        jnp.float32
    )
    chosen = jnp.dot(one_hot, strains, precision=highest)
    trace = lame_first * (chosen[:, 0] + chosen[:, 1] + chosen[:, 2])
    diagonal = jnp.asarray([1.0, 1.0, 1.0, 0.0, 0.0, 0.0], jnp.float32)
    stress = trace[:, None] * diagonal[None, :] + 2.0 * shear_mod * chosen
    plane = lax.axis_index(every).astype(jnp.float32)
    last = jnp.full((1, 12), plane, jnp.float32)
    return jnp.concatenate([jnp.concatenate([chosen, stress], axis=1), last], axis=0)


def shards(order_field, strains, variant_strain):
    length = order_field.shape[3]
    z_fwd, z_inv, y_both, x_fwd, x_inv = [jnp.asarray(t) for t in dft_tables(length)]
    coefs = coefficients(strains, variant_strain, 12)
    squares = None
    arrived = []
    for chunk in forward_chunks:
        sent, squares = call_z_forward(order_field, z_fwd, chunk, squares)
        arrived.append(exchange(after(sent, arrived)))
    specs = [
        call_xy_forward(block, y_both, x_fwd, chunk)
        for block, chunk in zip(arrived[:-1], forward_chunks)
    ]
    squares, arrived[-1], *specs = lax.optimization_barrier((squares, arrived[-1], *specs))
    partner = lax.ppermute(squares, "var", [(0, 1), (1, 0)])
    specs.append(call_xy_forward(arrived[-1], y_both, x_fwd, forward_chunks[-1]))
    resps = call_mix(coefs, specs, length)
    sends = []
    for resp, chunk in zip(resps, backward_chunks):
        sends.append(call_xy_back(resp, x_inv, y_both, chunk))
    sends[0], partner = lax.optimization_barrier((sends[0], partner))
    result = None
    returned = []
    for send, chunk in zip(sends, backward_chunks):
        returned.append(exchange(after(send, returned)))
        block = returned[-1]
        result = call_z_back(
            block, order_field, squares, partner, z_inv, chunk, result
        )
    return result


def solution(mesh):
    placed = (P("var", "py", "pz", None), P(), P())
    return jax.shard_map(
        shards, mesh=mesh, in_specs=placed, out_specs=P("var", "py", "pz", None), check_vma=False
    )
```

time: 733 us -> 254 us (0.35); the launches traced: 723 us -> 253 us
  waiting for transfers between devices: 342 us -> 138 us
  matrix products: 203 us -> 0.19 us
  local copies, waits for them, and re-layouts: 93.5 us -> 13.2 us
  Pallas kernels: 0 us -> 71.9 us
  other arithmetic: 29.5 us -> 0.16 us
  between operations: 14 us -> 0.16 us
  starting transfers between devices: 41.2 us -> 28.6 us
    dot_general x24 -> x1, matrix products: 203 us -> 0.19 us  [coefficients(): chosen = jnp.dot(one_hot, strains, precision=highest)]
    reduce_scatter x2 -> x0, waiting for transfers between devices: 145 us -> none  [the longest x1 78.7 us: shards(): lax.psum_scatter(mix_imag, 'var', scatter_dimension=0, tiled=True)]
    psum x1 -> x0, waiting for transfers between devices: 102 us -> none  [shards(): shared_real, shared_imag = lax.psum((shared_real, shared_imag), 'var')]
    pallas_call x0 -> x9, Pallas kernels: none -> 71.9 us  [the longest x2 16.9 us: call_xy_back(): pl.pallas_call(xy_back, grid=(count, 2), in_specs=[pl.BlockSpec((None, No...]
    reshape x7 -> x0, local copies, waits for them, and re-layouts: 69.5 us -> none  [the longest x2 23.5 us: shards(): resp_real.reshape(flat_shape)]
    all_to_all x4, waiting for transfers between devices: 94.8 us -> 138 us  [exchange(): return lax.all_to_all(block, every, split_axis=0, concat_axis=0, tiled=True)]
    mul x9 -> x1, other arithmetic: 17.7 us -> 0.01 us  [coefficients(): stress = trace[:, None] * diagonal[None, :] + 2.0 * shear_mod * chosen]
    dot_general x2 -> x1, local copies, waits for them, and re-layouts: 13.2 us -> 0.09 us  [coefficients(): chosen = jnp.dot(one_hot, strains, precision=highest)]
  transfers between devices with their start and end apart: 7 -> 5, of which waited for: 7 -> 4; matrix products, arithmetic and copies ran while one was open for 24% -> 0% of each run, Pallas kernels for 0% -> 21%
where the time goes in v1:
time: 254 us; the launch traced here: 253 us
  waiting for transfers between devices  138 us (54%)
  Pallas kernels  71.9 us (28%)
  starting transfers between devices  28.6 us (11%)
  local copies, waits for them, and re-layouts  13.2 us (5%)
    all_to_all x4, waiting for transfers between devices, exchange(): return lax.all_to_all(block, every, split_axis=0, concat_axis=0, tiled=True)  138 us
    all_to_all x4, starting transfers between devices, exchange(): return lax.all_to_all(block, every, split_axis=0, concat_axis=0, tiled=True)  28.1 us
    pallas_call x2, Pallas kernels, call_xy_back(): pl.pallas_call(xy_back, grid=(count, 2), in_specs=[pl.BlockSpec((None, No...  16.9 us
    pallas_call x2, Pallas kernels, call_xy_forward(): pl.pallas_call(xy_forward, grid=(count, 2), in_specs=[pl.BlockSpec((64, 3...  16 us
    pallas_call x2, Pallas kernels, call_z_back(): pl.pallas_call(z_back, grid=(4, count), in_specs=specs, out_specs=pl.Bloc...  15.2 us
    unnamed x36, local copies, waits for them, and re-layouts  13.1 us
    pallas_call x2, Pallas kernels, call_z_forward(): pl.pallas_call(z_forward, grid=(4, count), in_specs=[pl.BlockSpec((2, 32,...  13.1 us
    pallas_call x1, Pallas kernels, call_mix(): pl.pallas_call(body, grid=(length // rows,), in_specs=[pl.BlockSpec(memor...  10.7 us
  transfers between devices with their start and end apart: 5, of which 4 were waited for; matrix products, arithmetic and copies ran while one was open for 0% of the time, Pallas kernels for 21%

profile of v1, /device:TPU:1, one launch (start us, length us, event | category | flops | bytes accessed | tf_op | source)
XLA Modules:
  0.0 252.5 jit_solution(9142855106976478479)
XLA Ops:
  1.0 7.9 %z_forward.2 = (f32[128,64,128]{2,1,0:T(8,128)S(1)}, f32[32,32,256]{2,1,0:T(8,128)S(1)}) custom-call(f32[6,32,32,256]{3,2,1,0:T(8,128)} %phi_ref.3, f32[6,32,32,256]{3,2,1,0:T(8,128)} %phi_ref.3, bf16[256,768]{1,0:T(8,128)(2,1)S(1)} %copy-done.6), custom_call_target="tpu_custom_call" | custom-call | flops 1620000000 | bytes 8388608 | tf_op jit(solution)/shard_map/z_forward/pallas_call | solution.py:297
  9.0 2.0 copy-done.4
  11.0 12.0 %all-to-all-start = ((f32[128,64,128]{2,1,0:T(8,128)}), f32[128,64,128]{2,1,0:T(8,128)}, u32[]{:S(2)}, u32[]{:S(2)}) async-start(f32[128,64,128]{2,1,0:T(8,128)} %copy-done.4), calls=%async_computation | async-start | bytes 8388608 | tf_op jit(solution)/shard_map/all_to_all | solution.py:421
  22.9 5.1 %z_forward.3 = (f32[128,32,128]{2,1,0:T(8,128)}, f32[32,32,256]{2,1,0:T(8,128)S(1)}) custom-call(f32[6,32,32,256]{3,2,1,0:T(8,128)} %phi_ref.3, f32[6,32,32,256]{3,2,1,0:T(8,128)} %phi_ref.3, bf16[256,768]{1,0:T(8,128)(2,1)S(1)} %copy-done.7, f32[32,32,256]{2,1,0:T(8,128)S(1)} %get-tuple-element.18.refs_0_), custom_call_target="tpu_custom_call" | custom-call | flops 810000000 | bytes 4194304 | tf_op jit(solution)/shard_map/z_forward/pallas_call | solution.py:297
  28.1 51.1 %all-to-all-done.in_ref = f32[128,64,128]{2,1,0:T(8,128)} async-done(((f32[128,64,128]{2,1,0:T(8,128)}), f32[128,64,128]{2,1,0:T(8,128)}, u32[]{:S(2)}, u32[]{:S(2)}) %all-to-all-start) | async-done | bytes 4194336 | tf_op jit(solution)/shard_map/all_to_all | solution.py:421
  79.2 6.0 %all-to-all-start.1 = ((f32[128,32,128]{2,1,0:T(8,128)}), f32[128,32,128]{2,1,0:T(8,128)}, u32[]{:S(2)}, u32[]{:S(2)}) async-start(f32[128,32,128]{2,1,0:T(8,128)} %get-tuple-element.22), calls=%async_computation.1 | async-start | bytes 4194304 | tf_op jit(solution)/shard_map/all_to_all | solution.py:421
  85.4 10.6 %xy_forward.2.refs_0_ = f32[2,2,2,256,512]{4,3,2,1,0:T(8,128)} custom-call(f32[128,64,128]{2,1,0:T(8,128)} %all-to-all-done.in_ref, bf16[512,768]{1,0:T(8,128)(2,1)S(1)} %copy-done.14, bf16[1536,512]{1,0:T(8,128)(2,1)S(1)} %copy-done.12), custom_call_target="tpu_custom_call" | custom-call | flops 6400000000 | bytes 8388608 | tf_op jit(solution)/shard_map/xy_forward/pallas_call | solution.py:322
  96.1 20.1 %all-to-all-done.1.in_ref = f32[128,32,128]{2,1,0:T(8,128)} async-done(((f32[128,32,128]{2,1,0:T(8,128)}), f32[128,32,128]{2,1,0:T(8,128)}, u32[]{:S(2)}, u32[]{:S(2)}) %all-to-all-start.1) | async-done | bytes 2097184 | tf_op jit(solution)/shard_map/all_to_all | solution.py:421
  116.8 1.4 copy-done.13
  118.2 5.4 %xy_forward.3.refs_1_ = f32[1,2,2,256,512]{4,3,2,1,0:T(8,128)S(1)} custom-call(f32[128,32,128]{2,1,0:T(8,128)} %all-to-all-done.1.in_ref, bf16[512,768]{1,0:T(8,128)(2,1)S(1)} %copy-done.14, bf16[1536,512]{1,0:T(8,128)(2,1)S(1)} %copy-done.13), custom_call_target="tpu_custom_call" | custom-call | flops 3200000000 | bytes 4194304 | tf_op jit(solution)/shard_map/xy_forward/pallas_call | solution.py:322
  123.7 10.7 %mixing.1 = (f32[1,2,2,256,512]{4,3,2,1,0:T(8,128)S(1)}, f32[2,2,2,256,512]{4,3,2,1,0:T(8,128)}) custom-call(f32[13,12]{1,0:T(8,128)S(1)} %select_maximum_fusion.coef_ref, f32[2,2,2,256,512]{4,3,2,1,0:T(8,128)} %xy_forward.2.refs_0_, f32[1,2,2,256,512]{4,3,2,1,0:T(8,128)S(1)} %xy_forward.3.refs_1_), custom_call_target="tpu_custom_call" | custom-call | flops 50000000 | bytes 12582912 | tf_op jit(solution)/shard_map/mixing/pallas_call | solution.py:358
  134.4 1.3 copy-done.9
  135.7 5.7 %xy_back.3 = f32[128,32,128]{2,1,0:T(8,128)S(1)} custom-call(f32[1,2,2,256,512]{4,3,2,1,0:T(8,128)} %copy-done.9, bf16[1536,512]{1,0:T(8,128)(2,1)S(1)} %copy-done.10, bf16[512,768]{1,0:T(8,128)(2,1)S(1)} %copy-done.14), custom_call_target="tpu_custom_call" | custom-call | flops 3200000000 | bytes 4194304 | tf_op jit(solution)/shard_map/xy_back/pallas_call | solution.py:374
  141.4 1.3 copy-done.5
  143.8 5.2 %all-to-all-start.2 = ((f32[128,32,128]{2,1,0:T(8,128)}), f32[128,32,128]{2,1,0:T(8,128)S(1)}, u32[]{:S(2)}, u32[]{:S(2)}) async-start(f32[128,32,128]{2,1,0:T(8,128)} %copy-done.5), calls=%async_computation.2 | async-start | bytes 4194304 | tf_op jit(solution)/shard_map/all_to_all | solution.py:421
  149.0 1.4 copy-done.11
  151.6 11.2 %xy_back.2 = f32[128,64,128]{2,1,0:T(8,128)} custom-call(f32[2,2,2,256,512]{4,3,2,1,0:T(8,128)} %get-tuple-element.25.in_ref, bf16[1536,512]{1,0:T(8,128)(2,1)S(1)} %copy-done.11, bf16[512,768]{1,0:T(8,128)(2,1)S(1)} %copy-done.15), custom_call_target="tpu_custom_call" | custom-call | flops 6400000000 | bytes 8388608 | tf_op jit(solution)/shard_map/xy_back/pallas_call | solution.py:374
  162.8 17.4 %all-to-all-done.2.spec_ref = f32[128,32,128]{2,1,0:T(8,128)S(1)} async-done(((f32[128,32,128]{2,1,0:T(8,128)}), f32[128,32,128]{2,1,0:T(8,128)S(1)}, u32[]{:S(2)}, u32[]{:S(2)}) %all-to-all-start.2) | async-done | bytes 2097184 | tf_op jit(solution)/shard_map/all_to_all | solution.py:421
  180.2 4.9 %all-to-all-start.3 = ((f32[128,64,128]{2,1,0:T(8,128)}), f32[128,64,128]{2,1,0:T(8,128)}, u32[]{:S(2)}, u32[]{:S(2)}) async-start(f32[128,64,128]{2,1,0:T(8,128)} %xy_back.2), calls=%async_computation.3 | async-start | bytes 8388608 | tf_op jit(solution)/shard_map/all_to_all | solution.py:421
  185.2 1.2 copy-done.2
  186.4 5.3 %z_back.2.rest_0_ = f32[6,32,32,256]{3,2,1,0:T(8,128)} custom-call(f32[128,32,128]{2,1,0:T(8,128)S(1)} %all-to-all-done.2.spec_ref, f32[6,32,32,256]{3,2,1,0:T(8,128)} %phi_ref.3, f32[32,32,256]{2,1,0:T(8,128)S(1)} %get-tuple-element.27.own_ref, f32[32,32,256]{2,1,0:T(8,128)S(1)} %copy-done.2, bf16[768,256]{1,0:T(8,128)(2,1)S(1)} %copy-done.8), custom_call_target="tpu_custom_call" | custom-call | flops 810000000 | bytes 6291456 | tf_op jit(solution)/shard_map/z_back/pallas_call | solution.py:406
  191.7 49.7 %all-to-all-done.3.spec_ref = f32[128,64,128]{2,1,0:T(8,128)} async-done(((f32[128,64,128]{2,1,0:T(8,128)}), f32[128,64,128]{2,1,0:T(8,128)}, u32[]{:S(2)}, u32[]{:S(2)}) %all-to-all-start.3) | async-done | bytes 4194336 | tf_op jit(solution)/shard_map/all_to_all | solution.py:421
  241.4 1.2 copy-done.3
  242.6 9.9 %z_back.3 = f32[6,32,32,256]{3,2,1,0:T(8,128)} custom-call(f32[128,64,128]{2,1,0:T(8,128)} %all-to-all-done.3.spec_ref, f32[6,32,32,256]{3,2,1,0:T(8,128)} %phi_ref.3, f32[32,32,256]{2,1,0:T(8,128)S(1)} %get-tuple-element.27.own_ref, f32[32,32,256]{2,1,0:T(8,128)S(1)} %copy-done.3, bf16[768,256]{1,0:T(8,128)(2,1)S(1)} %copy-done.8, ...), custom_call_target="tpu_custom_call", output_to_operand_aliasing={{}: (5, {})} | custom-call | flops 1620000000 | bytes 12582912 | tf_op jit(solution)/shard_map/z_back/pallas_call | solution.py:406
  (36 shorter events, 4.2 us)
Async XLA Ops:
  0.0 85.2 %copy-start = (f32[24,6]{0,1:T(8,128)S(1)}, f32[24,6]{0,1:T(8,128)}, u32[]{:S(2)}) copy-start(f32[24,6]{0,1:T(8,128)} %param.10) | copy-start | bytes 1732
  0.0 1.0 copy-start.6
  9.0 2.0 copy-start.4
  11.0 12.0 %copy-start.7 = (bf16[256,768]{1,0:T(8,128)(2,1)S(1)}, bf16[256,768]{1,0:T(8,128)(2,1)}, u32[]{:S(2)}) copy-start(bf16[256,768]{1,0:T(8,128)(2,1)} %constant.33.clone.table_ref) | copy-start | bytes 1179652
  11.0 68.2 %all-to-all-start = ((f32[128,64,128]{2,1,0:T(8,128)}), f32[128,64,128]{2,1,0:T(8,128)}, u32[]{:S(2)}, u32[]{:S(2)}) async-start(f32[128,64,128]{2,1,0:T(8,128)} %copy-done.4), calls=%async_computation | async-start | bytes 8388608 | tf_op jit(solution)/shard_map/all_to_all | solution.py:421
  28.1 57.1 %copy-start.17 = (s32[24]{0:T(128)S(1)}, s32[24]{0:T(128)}, u32[]{:S(2)}) copy-start(s32[24]{0:T(128)} %param.11) | copy-start | bytes 292
  28.1 57.3 %copy-start.12 = (bf16[1536,512]{1,0:T(8,128)(2,1)S(1)}, bf16[1536,512]{1,0:T(8,128)(2,1)}, u32[]{:S(2)}) copy-start(bf16[1536,512]{1,0:T(8,128)(2,1)} %constant.36.clone.x_ref) | copy-start | bytes 4718596
  28.1 57.3 %copy-start.14 = (bf16[512,768]{1,0:T(8,128)(2,1)S(1)}, bf16[512,768]{1,0:T(8,128)(2,1)}, u32[]{:S(2)}) copy-start(bf16[512,768]{1,0:T(8,128)(2,1)} %constant.35.clone.y_ref) | copy-start | bytes 2359300
  79.2 36.9 %all-to-all-start.1 = ((f32[128,32,128]{2,1,0:T(8,128)}), f32[128,32,128]{2,1,0:T(8,128)}, u32[]{:S(2)}, u32[]{:S(2)}) async-start(f32[128,32,128]{2,1,0:T(8,128)} %get-tuple-element.22), calls=%async_computation.1 | async-start | bytes 4194304 | tf_op jit(solution)/shard_map/all_to_all | solution.py:421
  85.4 31.3 %copy-start.16 = (f32[6]{0:T(128)S(1)}, f32[6]{0:T(128)}, u32[]{:S(2)}) copy-start(f32[6]{0:T(128)} %constant.38.clone) | copy-start | bytes 76
  116.1 26.6 %collective-permute-start = (f32[32,32,256]{2,1,0:T(8,128)S(1)}, f32[32,32,256]{2,1,0:T(8,128)S(1)}, u32[]{:S(2)}, u32[]{:S(2)}) collective-permute-start(f32[32,32,256]{2,1,0:T(8,128)S(1)} %get-tuple-element.27.own_ref), channel_id=1, source_target_pairs={{0,64},{64,0},{1,65},{65,1},{2,66},{66,2},{3,67},{67,3},{4,68},{68... | collective-permute-start | bytes 3145736 | tf_op jit(solution)/shard_map/ppermute | solution.py:457
  116.8 1.4 copy-start.13
  123.7 12.0 %copy-start.10 = (bf16[1536,512]{1,0:T(8,128)(2,1)S(1)}, bf16[1536,512]{1,0:T(8,128)(2,1)}, u32[]{:S(2)}) copy-start(bf16[1536,512]{1,0:T(8,128)(2,1)} %constant.37.clone.x_ref) | copy-start | bytes 4718596
  134.4 1.3 copy-start.9
  141.4 1.3 copy-start.5
  142.7 1.1 copy-start.1
  143.8 36.4 %all-to-all-start.2 = ((f32[128,32,128]{2,1,0:T(8,128)}), f32[128,32,128]{2,1,0:T(8,128)S(1)}, u32[]{:S(2)}, u32[]{:S(2)}) async-start(f32[128,32,128]{2,1,0:T(8,128)} %copy-done.5), calls=%async_computation.2 | async-start | bytes 4194304 | tf_op jit(solution)/shard_map/all_to_all | solution.py:421
  149.0 1.4 copy-start.11
  150.4 1.1 copy-start.15
  162.8 22.4 %copy-start.8 = (bf16[768,256]{1,0:T(8,128)(2,1)S(1)}, bf16[768,256]{1,0:T(8,128)(2,1)}, u32[]{:S(2)}) copy-start(bf16[768,256]{1,0:T(8,128)(2,1)} %constant.34.clone.table_ref) | copy-start | bytes 1179652
  180.2 61.2 %all-to-all-start.3 = ((f32[128,64,128]{2,1,0:T(8,128)}), f32[128,64,128]{2,1,0:T(8,128)}, u32[]{:S(2)}, u32[]{:S(2)}) async-start(f32[128,64,128]{2,1,0:T(8,128)} %xy_back.2), calls=%async_computation.3 | async-start | bytes 8388608 | tf_op jit(solution)/shard_map/all_to_all | solution.py:421
  185.2 1.2 copy-start.2
  241.4 1.2 copy-start.3

commit v2 on v1

v2 whole, which is shorter than its diff:
```python
import functools

import jax
import jax.numpy as jnp
import ml_dtypes
import numpy as np
from jax import lax
from jax.experimental import pallas as pl
from jax.experimental.pallas import tpu as pltpu
from jax.sharding import PartitionSpec as P

lame_first = 1.5
shear_mod = 1.0
relax_coef = 1.0 / 1.4
grad_coef = 0.5
mobility = 0.2
landau_cubic = 3.0
landau_quartic = 0.5
two_pi = 6.283185307179586
highest = lax.Precision.HIGHEST
every = ("var", "py", "pz")
vmem_bytes = 48 * 1024 * 1024

groups = 3


def split_table(table):
    high = table.astype(ml_dtypes.bfloat16)
    low = (table - high.astype(np.float64)).astype(ml_dtypes.bfloat16)
    return high, low


def left_table(table):
    return np.concatenate(split_table(table), axis=1)


def right_table(table):
    return np.concatenate(split_table(table), axis=0)


def complex_blocks(angles, sign):
    cos, sin = np.cos(angles), sign * np.sin(angles)
    table = np.empty((2, angles.shape[0], 2, angles.shape[1]))
    table[0, :, 0], table[0, :, 1] = cos, sin
    table[1, :, 0], table[1, :, 1] = -sin, cos
    return table


@functools.cache
def dft_tables(length):
    half = length // 2
    ids = np.arange(length)
    unit = 2.0 * np.pi / length
    angles = (ids[:, None] * ids[None, :] % length) * unit
    cos, sin = np.cos(angles), np.sin(angles)
    z_fwd = left_table(np.concatenate([cos[:half], -sin[:half]], axis=0))
    weight = np.where(np.arange(half) == 0, 1.0, 2.0)[:, None]
    z_back = right_table(np.concatenate([cos[:half] * weight, -sin[:half] * weight], axis=0))
    low = np.arange(half)
    blocks = 8
    width = length // blocks
    y_fwd, y_back, x_fwd, x_back = [], [], [], []
    for parity in range(2):
        y_ids = 2 * low + parity
        fwd = complex_blocks((y_ids[:, None] * low[None, :] % length) * unit, -1.0)
        fwd = fwd.reshape(2, blocks, width // 2, length)
        y_fwd.append(left_table(fwd.transpose(3, 1, 0, 2).reshape(length, length)))
        back = complex_blocks((low[:, None] * y_ids[None, :] % length) * unit, 1.0)
        back = back.reshape(length, 2, blocks, width // 2)
        y_back.append(left_table(back.transpose(2, 1, 3, 0).reshape(length, length)))
        x_ids = low.reshape(2, 2, width).transpose(1, 0, 2).reshape(half)
        k_ids = 2 * low + parity
        fwd = complex_blocks((x_ids[:, None] * k_ids[None, :] % length) * unit, -1.0)
        x_fwd.append(right_table(fwd.reshape(length, length)))
        back = complex_blocks((k_ids[:, None] * x_ids[None, :] % length) * unit, 1.0)
        x_back.append(right_table(back.reshape(length, length)))
    return z_fwd, z_back, np.stack(y_fwd), np.stack(y_back), np.stack(x_fwd), np.stack(x_back)


def split_value(value):
    high = value.astype(jnp.bfloat16)
    low = (value - high.astype(jnp.float32)).astype(jnp.bfloat16)
    return high, low


def as_left(value):
    high, low = split_value(value)
    return jnp.concatenate([high, low, high], axis=1)


def as_right_tr(value):
    high, low = split_value(value)
    return jnp.concatenate([high, high, low], axis=1)


def as_right(value):
    high, low = split_value(value)
    return jnp.concatenate([high, high, low], axis=0)


def left_rows(table):
    width = table.shape[1] // 2
    return jnp.concatenate([table, table[:, :width]], axis=1)


def right_rows(table):
    depth = table.shape[0] // 2
    return jnp.concatenate([table[:depth], table], axis=0)


def matmul(left, right):
    return lax.dot_general(
        left, right, (((1,), (0,)), ((), ())), preferred_element_type=jnp.float32
    )


def matmul_tr(left, right):
    return lax.dot_general(
        left, right, (((1,), (1,)), ((), ())), preferred_element_type=jnp.float32
    )


def lane_ids(rows):
    return lax.broadcasted_iota(jnp.int32, (rows, 128), 1)


def z_forward(first_ref, second_ref, table_ref, out_ref, sq_ref):
    group = pl.program_id(1)
    for side, ref in enumerate((first_ref, second_ref)):
        phi = ref[...]
        squares = phi[0] * phi[0] + phi[1] * phi[1]
        lanes = slice(side * 128, side * 128 + 128)
        sq_ref[:, :, lanes] = jnp.where(group > 0, sq_ref[:, :, lanes], 0.0) + squares

    row_refs = [first_ref.reshape(1024, 128), second_ref.reshape(1024, 128)]
    flat_ref = out_ref.reshape(2048, 128)
    for batch in range(4):
        block = jnp.concatenate(
            [
                jnp.concatenate(
                    [ref[pl.ds(batch * 4 + y, 64, stride=16), :] for ref in row_refs], axis=1
                )
                for y in range(4)
            ],
            axis=0,
        )
        spectrum = matmul_tr(left_rows(table_ref[...]), as_right_tr(block))
        for pair in range(2):
            for part in range(2):
                rows = pl.ds(part * 8 + batch * 2 + pair, 128, stride=16)
                flat_ref[rows, :] = spectrum[
                    part * 128 : part * 128 + 128, pair * 128 : pair * 128 + 128
                ]


def transform_there(in_ref, y_ref, x_ref, out_ref, left_ref):
    lanes = lane_ids(256)
    low_half = lanes < 64
    first_bit = lane_ids(128) // 32 % 2 == 0
    halves = []
    for pp in range(2):
        evens, odds = [], []
        for place in (pp, pp + 2):
            first = in_ref[place * 16 : place * 16 + 8].reshape(256, 128)
            second = in_ref[place * 16 + 8 : place * 16 + 16].reshape(256, 128)
            evens.append(jnp.where(low_half, first, pltpu.roll(second, 64, 1)))
            odds.append(jnp.where(low_half, pltpu.roll(first, 64, 1), second))
        even = matmul(left_rows(y_ref[0]), as_right(jnp.concatenate(evens, axis=1)))
        odd = matmul(left_rows(y_ref[1]), as_right(jnp.concatenate(odds, axis=1)))
        low, high = even + odd, even - odd
        halves.append(
            [
                [side[:, :128] + side[:, 128:], side[:, :128] - side[:, 128:]]
                for side in (low, high)
            ]
        )
    for parity in range(2):
        for side in range(2):
            for part in range(2):
                rows = slice(part * 128, part * 128 + 128)
                zero = halves[0][side][parity][rows]
                one = halves[1][side][parity][rows]
                values = (
                    jnp.where(first_bit, zero, pltpu.roll(one, 32, 1)),
                    jnp.where(first_bit, pltpu.roll(zero, 96, 1), one),
                )
                for v, value in enumerate(values):
                    high, low = split_value(value)
                    start = v * 256 + side * 128
                    for third, piece in enumerate((high, low, high)):
                        column = third * 256 + part * 128
                        left_ref[parity, start : start + 128, column : column + 128] = piece
    for parity in range(2):
        product = matmul(left_ref[parity], right_rows(x_ref[parity]))
        for v in range(2):
            out_ref[v, :, parity * 256 : parity * 256 + 256] = product[v * 256 : v * 256 + 256]


def transform_back(in_ref, x_ref, y_ref, out_ref):
    lanes = lane_ids(256)
    low_half = lanes < 64
    first_bit = lanes // 32 % 2 == 0
    products = []
    for parity in range(2):
        columns = slice(parity * 256, parity * 256 + 256)
        block = jnp.concatenate([in_ref[0, :, columns], in_ref[1, :, columns]], axis=0)
        products.append(matmul(as_left(block), right_rows(x_ref[parity])))
    for side in range(2):
        field = products[0] + products[1] if side == 0 else products[0] - products[1]
        evens, odds = ([], []), ([], [])
        for part in range(2):
            zero = field[:256, part * 128 : part * 128 + 128]
            one = field[256:, part * 128 : part * 128 + 128]
            merged = (
                jnp.where(first_bit, zero, pltpu.roll(one, 32, 1)),
                jnp.where(first_bit, pltpu.roll(zero, 96, 1), one),
            )
            for pp in range(2):
                evens[pp].append(merged[pp][:128] + merged[pp][128:])
                odds[pp].append(merged[pp][:128] - merged[pp][128:])
        results = []
        for parity, pieces in enumerate((evens, odds)):
            right = jnp.concatenate([jnp.concatenate(p, axis=0) for p in pieces], axis=1)
            results.append(matmul(left_rows(y_ref[parity]), as_right(right)))
        for pp in range(2):
            even = results[0][:, pp * 128 : pp * 128 + 128]
            odd = results[1][:, pp * 128 : pp * 128 + 128]
            start = (side * 2 + pp) * 16
            first = jnp.where(low_half, even, pltpu.roll(odd, 64, 1))
            second = jnp.where(low_half, pltpu.roll(even, 64, 1), odd)
            out_ref[start : start + 8] = first.reshape(8, 2, 16, 128)
            out_ref[start + 8 : start + 16] = second.reshape(8, 2, 16, 128)


def waves(row, wave_z, length):
    half = length // 2
    ky = lax.broadcasted_iota(jnp.int32, (8, length), 0) + row
    column = lax.broadcasted_iota(jnp.int32, (8, length), 1)
    kx = column % half * 2 + column // half
    wy = jnp.where(ky >= half, ky - length, ky).astype(jnp.float32)
    wx = jnp.where(kx >= half, kx - length, kx).astype(jnp.float32)
    wz = jnp.full((8, length), wave_z, jnp.float32)
    squared = wx * wx + wy * wy + wz * wz
    volume = 1.0 / float(length * length * length)
    keep = jnp.where((ky == half) | (kx == half), 0.0, volume)
    grad = keep * squared * (grad_coef * (two_pi / length) ** 2)
    return wx, wy, wz, squared, keep, join(grad, grad)


def pick(value, part):
    half = value.shape[1] // 4
    return jnp.concatenate(
        [value[:, c * half : (c + 1) * half] for c in (part, part + 2)], axis=1
    )


def join(real, imag):
    half = real.shape[1] // 2
    pieces = [real[:, :half], imag[:, :half], real[:, half:], imag[:, half:]]
    return jnp.concatenate(pieces, axis=1)


def driving(strain, wx, wy, wz, squared, keep):
    inverse = 1.0 / jnp.maximum(squared, 1.0)
    trace = lame_first * (strain[0] + strain[1] + strain[2])
    s11 = trace + 2.0 * shear_mod * strain[0]
    s22 = trace + 2.0 * shear_mod * strain[1]
    s33 = trace + 2.0 * shear_mod * strain[2]
    s23 = 2.0 * shear_mod * strain[3]
    s13 = 2.0 * shear_mod * strain[4]
    s12 = 2.0 * shear_mod * strain[5]
    t1 = (s11 * wx + s12 * wy + s13 * wz) * inverse
    t2 = (s12 * wx + s22 * wy + s23 * wz) * inverse
    t3 = (s13 * wx + s23 * wy + s33 * wz) * inverse
    normal = (wx * t1 + wy * t2 + wz * t3) * (relax_coef * inverse)
    u1 = t1 - normal * wx
    u2 = t2 - normal * wy
    u3 = t3 - normal * wz
    return [
        keep * (strain[0] - wx * u1),
        keep * (strain[1] - wy * u2),
        keep * (strain[2] - wz * u3),
        keep * (2.0 * strain[3] - (wy * u3 + wz * u2)),
        keep * (2.0 * strain[4] - (wx * u3 + wz * u1)),
        keep * (2.0 * strain[5] - (wx * u2 + wy * u1)),
    ]


def middle(coef_ref, in_hbm, yf_hbm, xf_hbm, xb_hbm, yb_hbm, out_hbm, *scratch):
    in_ref, yf_ref, xf_ref, xb_ref, yb_ref, field_ref, left_ref, out_ref, sems = scratch
    length = field_ref.shape[1]
    wave_z = coef_ref[12, 0]
    steps = groups * 2

    def part_of(ref, step):
        return ref.at[
            pl.ds(pl.multiple_of(step % 2 * 64, 64), 64),
            pl.ds(pl.multiple_of(step // 2 * 2, 2), 2),
        ]

    def arrival(step):
        slot = step % 2
        return pltpu.make_async_copy(part_of(in_hbm, step), in_ref.at[slot], sems.at[slot])

    def departure(step):
        slot = step % 2
        return pltpu.make_async_copy(out_ref.at[slot], part_of(out_hbm, step), sems.at[2 + slot])

    moves = [(yf_hbm, yf_ref), (xf_hbm, xf_ref), (xb_hbm, xb_ref), (yb_hbm, yb_ref)]
    copies = [
        pltpu.make_async_copy(source, target, sems.at[4 + number])
        for number, (source, target) in enumerate(moves)
    ]
    copies[0].start()
    arrival(0).start()
    for copy in copies[1:]:
        copy.start()
    copies[0].wait()
    copies[1].wait()

    def there(step, carry):
        @pl.when(step + 1 < steps)
        def _():
            arrival(step + 1).start()

        arrival(step).wait()
        transform_there(
            in_ref.at[step % 2], yf_ref, xf_ref, field_ref.at[pl.ds(step * 2, 2)], left_ref
        )
        return carry

    lax.fori_loop(0, steps, there, 0)
    places = [(p % 6 // 2 * 2 + p // 6) * 2 + p % 2 for p in range(12)]

    def tile(step, carry):
        row = pl.multiple_of(step * 8, 8)
        rows = pl.ds(row, 8)
        wx, wy, wz, squared, keep, grad = waves(row, wave_z, length)
        strains = None
        for q, place in enumerate(places):
            value = field_ref[place, rows, :]
            terms = [coef_ref[q, m] * value for m in range(6)]
            strains = terms if q == 0 else [total + term for total, term in zip(strains, terms)]
        parts = [
            driving([pick(total, part) for total in strains], wx, wy, wz, squared, keep)
            for part in range(2)
        ]
        drive = [join(parts[0][m], parts[1][m]) for m in range(6)]
        for p, place in enumerate(places):
            total = grad * field_ref[place, rows, :]
            for m in range(6):
                total = total + coef_ref[p, 6 + m] * drive[m]
            field_ref[place, rows, :] = total
        return carry

    lax.fori_loop(0, length // 8, tile, 0)
    copies[2].wait()
    copies[3].wait()

    def back(step, carry):
        @pl.when(step >= 2)
        def _():
            departure(step - 2).wait()

        transform_back(field_ref.at[pl.ds(step * 2, 2)], xb_ref, yb_ref, out_ref.at[step % 2])
        departure(step).start()
        return carry

    lax.fori_loop(0, steps, back, 0)
    departure(steps - 2).wait()
    departure(steps - 1).wait()


def z_back(spec_ref, phi_ref, own_ref, partner_ref, table_ref, out_ref, force_ref):
    flat_ref = spec_ref.reshape(2048, 128)
    row_refs = [force_ref.at[side].reshape(1024, 128) for side in range(2)]
    for batch in range(4):
        lefts = []
        for pair in range(2):
            turned = [
                flat_ref[pl.ds(part * 8 + batch * 2 + pair, 128, stride=16), :].T
                for part in range(2)
            ]
            lefts.append(jnp.concatenate(turned, axis=1))
        force = matmul(as_left(jnp.concatenate(lefts, axis=0)), right_rows(table_ref[...]))
        for y in range(4):
            rows = pl.ds(batch * 4 + y, 64, stride=16)
            for side, ref in enumerate(row_refs):
                lanes = slice(side * 128, side * 128 + 128)
                ref[rows, :] = force[y * 64 : y * 64 + 64, lanes]
    for side in range(2):
        lanes = slice(side * 128, side * 128 + 128)
        total_sq = own_ref[:, :, lanes] + partner_ref[:, :, lanes]
        for v in range(2):
            phi = phi_ref[v, :, :, lanes]
            chemical = phi - landau_cubic * phi * phi + landau_quartic * phi * total_sq
            out_ref[v, :, :, lanes] = phi - mobility * (chemical + force_ref[side, v])


def params(count):
    return pltpu.CompilerParams(
        dimension_semantics=("arbitrary",) * count, vmem_limit_bytes=vmem_bytes
    )


def cost(flops, moved):
    return pl.CostEstimate(flops=int(flops), bytes_accessed=int(moved), transcendentals=0)


def hbm(shape):
    return pltpu.HBM(shape, jnp.float32)


def in_hbm(array):
    return pltpu.with_memory_space_constraint(array, pltpu.HBM)


def whole(array):
    return pl.BlockSpec(array.shape, lambda *ids: (0,) * array.ndim)


group_bytes = 2 * 32 * 32 * 256 * 4


def call_z_forward(phi, table):
    return pl.pallas_call(
        z_forward,
        grid=(2, groups),
        in_specs=[
            pl.BlockSpec((2, 32, 16, 128), lambda j, g: (g, 0, j, 0)),
            pl.BlockSpec((2, 32, 16, 128), lambda j, g: (g, 0, j, 1)),
            whole(table),
        ],
        out_specs=[
            pl.BlockSpec((128, 2, 8, 128), lambda j, g: (0, g, j, 0)),
            pl.BlockSpec((32, 16, 256), lambda j, g: (0, j, 0)),
        ],
        out_shape=[hbm((128, 2 * groups, 16, 128)), hbm((32, 32, 256))],
        compiler_params=params(2),
        cost_estimate=cost(2.4e9, 2 * groups * group_bytes),
        name="z_forward",
    )(phi, phi, table)


smem = pl.BlockSpec(memory_space=pltpu.SMEM)
anywhere = pl.BlockSpec(memory_space=pl.ANY)


def call_middle(coefs, spec, tables):
    shapes = [
        pltpu.VMEM((2, 64, 2, 16, 128), jnp.float32),
        *[pltpu.VMEM(table.shape, jnp.bfloat16) for table in tables],
        pltpu.VMEM((4 * groups, 256, 512), jnp.float32),
        pltpu.VMEM((2, 512, 768), jnp.bfloat16),
        pltpu.VMEM((2, 64, 2, 16, 128), jnp.float32),
        pltpu.SemaphoreType.DMA((8,)),
    ]
    return pl.pallas_call(
        middle,
        in_specs=[smem] + [anywhere] * (1 + len(tables)),
        out_specs=anywhere,
        out_shape=hbm(spec.shape),
        scratch_shapes=shapes,
        compiler_params=pltpu.CompilerParams(vmem_limit_bytes=vmem_bytes),
        cost_estimate=cost(20e9, 6 * groups * group_bytes),
        name="middle",
    )(coefs, spec, *tables)


def call_z_back(spec, phi, own, partner, table):
    return pl.pallas_call(
        z_back,
        grid=(2, groups),
        in_specs=[
            pl.BlockSpec((128, 2, 8, 128), lambda j, g: (0, g, j, 0)),
            pl.BlockSpec((2, 32, 16, 256), lambda j, g: (g, 0, j, 0)),
            pl.BlockSpec((32, 16, 256), lambda j, g: (0, j, 0)),
            pl.BlockSpec((32, 16, 256), lambda j, g: (0, j, 0)),
            whole(table),
        ],
        out_specs=pl.BlockSpec((2, 32, 16, 256), lambda j, g: (g, 0, j, 0)),
        out_shape=hbm(phi.shape),
        scratch_shapes=[pltpu.VMEM((2, 2, 32, 16, 128), jnp.float32)],
        compiler_params=params(2),
        cost_estimate=cost(2.4e9, 3 * groups * group_bytes),
        name="z_back",
    )(spec, phi, in_hbm(own), in_hbm(partner), table)


def exchange(block):
    return lax.all_to_all(block, every, split_axis=0, concat_axis=0, tiled=True)


def coefficients(strains, variant_strain, variants):
    bank_rows = strains.shape[0]
    picked = variant_strain[:variants]
    one_hot = (picked[:, None] == jnp.arange(bank_rows, dtype=jnp.int32)[None, :]).astype(
        jnp.float32
    )
    chosen = jnp.dot(one_hot, strains, precision=highest)
    trace = lame_first * (chosen[:, 0] + chosen[:, 1] + chosen[:, 2])
    diagonal = jnp.asarray([1.0, 1.0, 1.0, 0.0, 0.0, 0.0], jnp.float32)
    stress = trace[:, None] * diagonal[None, :] + 2.0 * shear_mod * chosen
    plane = lax.axis_index(every).astype(jnp.float32)
    last = jnp.full((1, 12), plane, jnp.float32)
    return jnp.concatenate([jnp.concatenate([chosen, stress], axis=1), last], axis=0)


def shards(order_field, strains, variant_strain):
    length = order_field.shape[3]
    tables = [in_hbm(jnp.asarray(table)) for table in dft_tables(length)]
    z_fwd, z_inv, y_fwd, y_inv, x_fwd, x_inv = tables
    coefs = coefficients(strains, variant_strain, 12)
    sent, squares = call_z_forward(order_field, z_fwd)
    arrived = exchange(sent)
    squares, arrived = lax.optimization_barrier((squares, arrived))
    partner = lax.ppermute(squares, "var", [(0, 1), (1, 0)])
    sent = call_middle(coefs, arrived, (y_fwd, x_fwd, x_inv, y_inv))
    sent, partner = lax.optimization_barrier((sent, partner))
    returned = exchange(sent)
    return call_z_back(returned, order_field, squares, partner, z_inv)


def solution(mesh):
    placed = (P("var", "py", "pz", None), P(), P())
    return jax.shard_map(
        shards, mesh=mesh, in_specs=placed, out_specs=P("var", "py", "pz", None), check_vma=False
    )
```

time: 254 us -> 234 us (0.921)
  blocking collectives: 0 us -> 90.1 us
  waiting for transfers between devices: 138 us -> 80.5 us
  Pallas kernels: 71.9 us -> 50.4 us
  starting transfers between devices: 28.6 us -> 11.9 us
  local copies, waits for them, and re-layouts: 13.2 us -> 0.12 us
    all_to_all x0 -> x1, blocking collectives: none -> 90.1 us  [exchange(): return lax.all_to_all(block, every, split_axis=0, concat_axis=0, tiled=True)]
    all_to_all x4 -> x1, waiting for transfers between devices: 138 us -> 80.5 us  [exchange(): return lax.all_to_all(block, every, split_axis=0, concat_axis=0, tiled=True)]
    pallas_call x9 -> x3, Pallas kernels: 71.9 us -> 50.4 us  [the longest x1 27.8 us: call_middle(): pl.pallas_call(middle, in_specs=[smem] + [anywhere] * (1 + len(tables)),...]
    all_to_all x4 -> x1, starting transfers between devices: 28.1 us -> 11.9 us  [exchange(): return lax.all_to_all(block, every, split_axis=0, concat_axis=0, tiled=True)]
    unnamed x36 -> x10, local copies, waits for them, and re-layouts: 13.1 us -> 0.02 us
  transfers between devices with their start and end apart: 5 -> 2, of which waited for: 4 -> 1; matrix products, arithmetic and copies ran while one was open for 0% -> 0% of each run, Pallas kernels for 21% -> 12%
where the time goes in v2:
time: 234 us; the launch traced here: 233 us
  blocking collectives  90.1 us (39%)
  waiting for transfers between devices  80.5 us (34%)
  Pallas kernels  50.4 us (22%)
  starting transfers between devices  11.9 us (5%)
    all_to_all x1, blocking collectives, exchange(): return lax.all_to_all(block, every, split_axis=0, concat_axis=0, tiled=True)  90.1 us
    all_to_all x1, waiting for transfers between devices, exchange(): return lax.all_to_all(block, every, split_axis=0, concat_axis=0, tiled=True)  80.5 us
    pallas_call x1, Pallas kernels, call_middle(): pl.pallas_call(middle, in_specs=[smem] + [anywhere] * (1 + len(tables)),...  27.8 us
    pallas_call x1, Pallas kernels, call_z_back(): pl.pallas_call(z_back, grid=(2, groups), in_specs=[pl.BlockSpec((128, 2,...  12.3 us
    all_to_all x1, starting transfers between devices, exchange(): return lax.all_to_all(block, every, split_axis=0, concat_axis=0, tiled=True)  11.9 us
    pallas_call x1, Pallas kernels, call_z_forward(): pl.pallas_call(z_forward, grid=(2, groups), in_specs=[pl.BlockSpec((2, 32...  10.3 us
  transfers between devices with their start and end apart: 2, of which 1 were waited for; matrix products, arithmetic and copies ran while one was open for 0% of the time, Pallas kernels for 12%

profile of v2, /device:TPU:1, one launch (start us, length us, event | category | flops | bytes accessed | tf_op | source)
XLA Modules:
  0.0 233.4 jit_solution(6552368466977426981)
XLA Ops:
  0.0 0.0 copy-start
  0.0 10.3 %z_forward.1 = (f32[128,6,16,128]{3,2,1,0:T(8,128)}, f32[32,32,256]{2,1,0:T(8,128)}) custom-call(f32[6,32,32,256]{3,2,1,0:T(8,128)} %phi_ref.1, f32[6,32,32,256]{3,2,1,0:T(8,128)} %phi_ref.1, bf16[256,512]{1,0:T(8,128)(2,1)} %constant.35.clone.table_ref), custom_call_target="tpu_custom_call" | custom-call | flops 2400000000 | bytes 12582912 | tf_op jit(solution)/shard_map/z_forward/pallas_call | solution.py:426
  10.3 0.0 copy-start.4
  10.3 0.0 copy-start.3
  10.3 0.0 copy-start.1
  10.3 11.9 %all-to-all-start = ((f32[128,6,16,128]{3,2,1,0:T(8,128)}), f32[128,6,16,128]{3,2,1,0:T(8,128)}, u32[]{:S(2)}, u32[]{:S(2)}) async-start(f32[128,6,16,128]{3,2,1,0:T(8,128)} %get-tuple-element.12), calls=%async_computation | async-start | bytes 12582912 | tf_op jit(solution)/shard_map/all_to_all | solution.py:491
  22.2 0.0 copy-done
  22.3 0.0 copy-done.4
  22.3 0.2 fusion
  22.5 0.1 copy.15
  22.6 0.0 copy-done.3
  22.6 0.1 multiply_add_fusion
  22.6 0.1 select_maximum_fusion.coef_ref
  22.7 80.5 %all-to-all-done.in_hbm = f32[128,6,16,128]{3,2,1,0:T(8,128)} async-done(((f32[128,6,16,128]{3,2,1,0:T(8,128)}), f32[128,6,16,128]{3,2,1,0:T(8,128)}, u32[]{:S(2)}, u32[]{:S(2)}) %all-to-all-start) | async-done | bytes 6291488 | tf_op jit(solution)/shard_map/all_to_all | solution.py:491
  103.2 0.0 copy-done.1
  103.2 0.0 collective-permute-start
  103.2 27.8 %middle.1 = f32[128,6,16,128]{3,2,1,0:T(8,128)} custom-call(f32[13,12]{1,0:T(8,128)S(1)} %select_maximum_fusion.coef_ref, f32[128,6,16,128]{3,2,1,0:T(8,128)} %all-to-all-done.in_hbm, bf16[2,256,512]{2,1,0:T(8,128)(2,1)} %constant.37.clone.yf_hbm, bf16[2,512,256]{2,1,0:T(8,128)(2,1)} %constant.39.clone.xf_hbm, bf16[2,512,256]{2,1,0:T(8,128)(2,1)} %constant.40.clone.xb_hbm, ...), custom_call_target="tpu_custom_call" | custom-call | flops 20000000000 | bytes 37748736 | tf_op jit(solution)/shard_map/middle/pallas_call | solution.py:458
  131.0 0.0 collective-permute-done.partner_ref
  131.0 0.0 copy-start.2
  131.0 90.1 %all_to_all.10.spec_ref = f32[128,6,16,128]{3,2,1,0:T(8,128)} all-to-all(f32[128,6,16,128]{3,2,1,0:T(8,128)} %middle.1), channel_id=1, replica_groups=mesh['var'=2,'py'=8,'pz'=8] {'var','py','pz'}, dimensions={0} | all-to-all | bytes 12582912 | tf_op jit(solution)/shard_map/all_to_all | solution.py:491
  221.1 0.0 copy-done.2
  221.1 12.3 %z_back.1 = f32[6,32,32,256]{3,2,1,0:T(8,128)} custom-call(f32[128,6,16,128]{3,2,1,0:T(8,128)} %all_to_all.10.spec_ref, f32[6,32,32,256]{3,2,1,0:T(8,128)} %phi_ref.1, f32[32,32,256]{2,1,0:T(8,128)} %get-tuple-element.14.own_ref, f32[32,32,256]{2,1,0:T(8,128)} %copy-done.2, bf16[512,256]{1,0:T(8,128)(2,1)} %constant.36.clone.table_ref), custom_call_target="tpu_custom_call" | custom-call | flops 2400000000 | bytes 18874368 | tf_op jit(solution)/shard_map/z_back/pallas_call | solution.py:471
  (1 shorter events, 0.0 us)
Async XLA Ops:
  0.0 22.2 %copy-start = (f32[24,6]{0,1:T(8,128)S(1)}, f32[24,6]{0,1:T(8,128)}, u32[]{:S(2)}) copy-start(f32[24,6]{0,1:T(8,128)} %param.11) | copy-start | bytes 1732
  10.3 11.9 %copy-start.4 = (s32[24]{0:T(128)S(1)}, s32[24]{0:T(128)}, u32[]{:S(2)}) copy-start(s32[24]{0:T(128)} %param.12) | copy-start | bytes 292
  10.3 12.3 %copy-start.3 = (f32[6]{0:T(128)S(1)}, f32[6]{0:T(128)}, u32[]{:S(2)}) copy-start(f32[6]{0:T(128)} %constant.41.clone) | copy-start | bytes 76
  10.3 92.9 %copy-start.1 = (f32[32,32,256]{2,1,0:T(8,128)S(1)}, f32[32,32,256]{2,1,0:T(8,128)}, u32[]{:S(2)}) copy-start(f32[32,32,256]{2,1,0:T(8,128)} %get-tuple-element.14.own_ref) | copy-start | bytes 3145732
  10.3 92.8 %all-to-all-start = ((f32[128,6,16,128]{3,2,1,0:T(8,128)}), f32[128,6,16,128]{3,2,1,0:T(8,128)}, u32[]{:S(2)}, u32[]{:S(2)}) async-start(f32[128,6,16,128]{3,2,1,0:T(8,128)} %get-tuple-element.12), calls=%async_computation | async-start | bytes 12582912 | tf_op jit(solution)/shard_map/all_to_all | solution.py:491
  103.2 27.8 %collective-permute-start = (f32[32,32,256]{2,1,0:T(8,128)S(1)}, f32[32,32,256]{2,1,0:T(8,128)S(1)}, u32[]{:S(2)}, u32[]{:S(2)}) collective-permute-start(f32[32,32,256]{2,1,0:T(8,128)S(1)} %copy-done.1), channel_id=1, source_target_pairs={{0,64},{64,0},{1,65},{65,1},{2,66},{66,2},{3,67},{67,3},{4,68},{68... | collective-permute-start | bytes 3145736 | tf_op jit(solution)/shard_map/ppermute | solution.py:517
  131.0 90.1 %copy-start.2 = (f32[32,32,256]{2,1,0:T(8,128)}, f32[32,32,256]{2,1,0:T(8,128)S(1)}, u32[]{:S(2)}) copy-start(f32[32,32,256]{2,1,0:T(8,128)S(1)} %collective-permute-done.partner_ref) | copy-start | bytes 3145732

commit v3 on v2

--- a/solution.py
+++ b/solution.py
@@ -18,7 +18,7 @@
 landau_quartic = 0.5
 two_pi = 6.283185307179586
 highest = lax.Precision.HIGHEST
-every = ("var", "py", "pz")
+every = ("var", "pz", "py")
 vmem_bytes = 48 * 1024 * 1024
 
 groups = 3
@@ -54,7 +54,7 @@
     angles = (ids[:, None] * ids[None, :] % length) * unit
     cos, sin = np.cos(angles), np.sin(angles)
     z_fwd = left_table(np.concatenate([cos[:half], -sin[:half]], axis=0))
-    weight = np.where(np.arange(half) == 0, 1.0, 2.0)[:, None]
+    weight = -mobility * np.where(np.arange(half) == 0, 1.0, 2.0)[:, None]
     z_back = right_table(np.concatenate([cos[:half] * weight, -sin[:half] * weight], axis=0))
     low = np.arange(half)
     blocks = 8
@@ -124,33 +124,76 @@
     return lax.broadcasted_iota(jnp.int32, (rows, 128), 1)
 
 
-def z_forward(first_ref, second_ref, table_ref, out_ref, sq_ref):
-    group = pl.program_id(1)
-    for side, ref in enumerate((first_ref, second_ref)):
-        phi = ref[...]
-        squares = phi[0] * phi[0] + phi[1] * phi[1]
-        lanes = slice(side * 128, side * 128 + 128)
-        sq_ref[:, :, lanes] = jnp.where(group > 0, sq_ref[:, :, lanes], 0.0) + squares
-
-    row_refs = [first_ref.reshape(1024, 128), second_ref.reshape(1024, 128)]
-    flat_ref = out_ref.reshape(2048, 128)
-    for batch in range(4):
-        block = jnp.concatenate(
-            [
-                jnp.concatenate(
-                    [ref[pl.ds(batch * 4 + y, 64, stride=16), :] for ref in row_refs], axis=1
-                )
-                for y in range(4)
-            ],
-            axis=0,
-        )
-        spectrum = matmul_tr(left_rows(table_ref[...]), as_right_tr(block))
-        for pair in range(2):
-            for part in range(2):
-                rows = pl.ds(part * 8 + batch * 2 + pair, 128, stride=16)
-                flat_ref[rows, :] = spectrum[
-                    part * 128 : part * 128 + 128, pair * 128 : pair * 128 + 128
-                ]
+def z_pieces(spec_hbm, spec_ref, grid_hbm, grid_ref, sems):
+    def spec(step, back):
+        group, part = step // 2 * 2, pl.multiple_of(step % 2 * 8, 8)
+        place = (slice(None), pl.ds(group, 2), pl.ds(part, 8))
+        ends = [spec_hbm.at[place], spec_ref.at[step, :, pl.ds(0, 2)]]
+        return pltpu.make_async_copy(*(ends[::-1] if back else ends), sems.at[0, step])
+
+    def grid(step, side, back):
+        group, part = step // 2 * 2, pl.multiple_of(step % 2 * 16, 16)
+        place = (pl.ds(group, 2), slice(None), pl.ds(part, 16))
+        ends = [
+            grid_hbm.at[place + (pl.ds(side * 128, 128),)],
+            grid_ref.at[step, side, :, :, pl.ds(0, 16)],
+        ]
+        number = (2 if back else 0) + 1 + side
+        return pltpu.make_async_copy(*(ends[::-1] if back else ends), sems.at[number, step])
+
+    return spec, grid
+
+
+def z_forward(table_ref, phi_hbm, out_hbm, sq_hbm, phi_ref, out_ref, sq_ref, sems):
+    spec, grid = z_pieces(out_hbm, out_ref, phi_hbm, phi_ref, sems)
+    steps = groups * 2
+    for step in range(steps):
+        for side in range(2):
+            grid(step, side, False).start()
+    sq_ref[...] = jnp.zeros_like(sq_ref)
+    rows_ref = phi_ref.reshape(steps * 3072, 128)
+    flat_ref = out_ref.reshape(steps * 3072, 128)
+
+    def body(step, carry):
+        part_y = step % 2
+        for side in range(2):
+            grid(step, side, False).wait()
+        base = pl.multiple_of(step * 3072, 8)
+        for batch in range(4):
+            block = jnp.concatenate(
+                [
+                    jnp.concatenate(
+                        [
+                            rows_ref[pl.ds(base + side * 1536 + batch * 4 + y, 64, stride=24), :]
+                            for side in range(2)
+                        ],
+                        axis=1,
+                    )
+                    for y in range(4)
+                ],
+                axis=0,
+            )
+            spectrum = matmul_tr(left_rows(table_ref[...]), as_right_tr(block))
+            for pair in range(2):
+                for part in range(2):
+                    start = base + part * 8 + batch * 2 + pair
+                    flat_ref[pl.ds(start, 128, stride=24), :] = spectrum[
+                        part * 128 : part * 128 + 128, pair * 128 : pair * 128 + 128
+                    ]
+        spec(step, True).start()
+        ys = pl.ds(pl.multiple_of(part_y * 16, 16), 16)
+        for side in range(2):
+            lanes = slice(side * 128, side * 128 + 128)
+            one, two = [phi_ref[step, side, v, :, 0:16, :] for v in range(2)]
+            sq_ref[:, ys, lanes] += one * one + two * two
+        return carry
+
+    lax.fori_loop(0, steps, body, 0)
+    last = pltpu.make_async_copy(sq_ref, sq_hbm, sems.at[3, 0])
+    last.start()
+    for step in range(steps):
+        spec(step, True).wait()
+    last.wait()
 
 
 def transform_there(in_ref, y_ref, x_ref, out_ref, left_ref):
@@ -161,8 +204,12 @@
     for pp in range(2):
         evens, odds = [], []
         for place in (pp, pp + 2):
-            first = in_ref[place * 16 : place * 16 + 8].reshape(256, 128)
-            second = in_ref[place * 16 + 8 : place * 16 + 16].reshape(256, 128)
+            first, second = [
+                jnp.concatenate(
+                    [in_ref[pz * 8 + place * 2 + side].reshape(32, 128) for pz in range(8)], axis=0
+                )
+                for side in range(2)
+            ]
             evens.append(jnp.where(low_half, first, pltpu.roll(second, 64, 1)))
             odds.append(jnp.where(low_half, pltpu.roll(first, 64, 1), second))
         even = matmul(left_rows(y_ref[0]), as_right(jnp.concatenate(evens, axis=1)))
@@ -225,11 +272,13 @@
         for pp in range(2):
             even = results[0][:, pp * 128 : pp * 128 + 128]
             odd = results[1][:, pp * 128 : pp * 128 + 128]
-            start = (side * 2 + pp) * 16
+            place = (side * 2 + pp) * 2
             first = jnp.where(low_half, even, pltpu.roll(odd, 64, 1))
             second = jnp.where(low_half, pltpu.roll(even, 64, 1), odd)
-            out_ref[start : start + 8] = first.reshape(8, 2, 16, 128)
-            out_ref[start + 8 : start + 16] = second.reshape(8, 2, 16, 128)
+            for pz in range(8):
+                rows = slice(pz * 32, pz * 32 + 32)
+                out_ref[pz * 8 + place] = first[rows].reshape(2, 16, 128)
+                out_ref[pz * 8 + place + 1] = second[rows].reshape(2, 16, 128)
 
 
 def waves(row, wave_z, length):
@@ -371,30 +420,51 @@
     departure(steps - 1).wait()
 
 
-def z_back(spec_ref, phi_ref, own_ref, partner_ref, table_ref, out_ref, force_ref):
-    flat_ref = spec_ref.reshape(2048, 128)
-    row_refs = [force_ref.at[side].reshape(1024, 128) for side in range(2)]
-    for batch in range(4):
-        lefts = []
-        for pair in range(2):
-            turned = [
-                flat_ref[pl.ds(part * 8 + batch * 2 + pair, 128, stride=16), :].T
-                for part in range(2)
-            ]
-            lefts.append(jnp.concatenate(turned, axis=1))
-        force = matmul(as_left(jnp.concatenate(lefts, axis=0)), right_rows(table_ref[...]))
-        for y in range(4):
-            rows = pl.ds(batch * 4 + y, 64, stride=16)
-            for side, ref in enumerate(row_refs):
-                lanes = slice(side * 128, side * 128 + 128)
-                ref[rows, :] = force[y * 64 : y * 64 + 64, lanes]
-    for side in range(2):
-        lanes = slice(side * 128, side * 128 + 128)
-        total_sq = own_ref[:, :, lanes] + partner_ref[:, :, lanes]
-        for v in range(2):
-            phi = phi_ref[v, :, :, lanes]
-            chemical = phi - landau_cubic * phi * phi + landau_quartic * phi * total_sq
-            out_ref[v, :, :, lanes] = phi - mobility * (chemical + force_ref[side, v])
+def local_part(phi_ref, own_ref, partner_ref, out_ref):
+    phi = phi_ref[...]
+    total_sq = own_ref[...] + partner_ref[...]
+    chemical = phi - landau_cubic * phi * phi + landau_quartic * phi * total_sq[None]
+    out_ref[...] = phi - mobility * chemical
+
+
+def z_back(table_ref, spec_hbm, base_hbm, out_hbm, spec_ref, base_ref, sems):
+    spec, grid = z_pieces(spec_hbm, spec_ref, base_hbm, base_ref, sems)
+    grid_out = z_pieces(spec_hbm, spec_ref, out_hbm, base_ref, sems)[1]
+    steps = groups * 2
+    for step in range(steps):
+        spec(step, False).start()
+        for side in range(2):
+            grid(step, side, False).start()
+    flat_ref = spec_ref.reshape(steps * 3072, 128)
+    rows_ref = base_ref.reshape(steps * 3072, 128)
+
+    def body(step, carry):
+        base = pl.multiple_of(step * 3072, 8)
+        spec(step, False).wait()
+        for side in range(2):
+            grid(step, side, False).wait()
+        for batch in range(4):
+            lefts = []
+            for pair in range(2):
+                turned = []
+                for part in range(2):
+                    start = base + part * 8 + batch * 2 + pair
+                    turned.append(flat_ref[pl.ds(start, 128, stride=24), :].T)
+                lefts.append(jnp.concatenate(turned, axis=1))
+            force = matmul(as_left(jnp.concatenate(lefts, axis=0)), right_rows(table_ref[...]))
+            for y in range(4):
+                for side in range(2):
+                    rows = pl.ds(base + side * 1536 + batch * 4 + y, 64, stride=24)
+                    lanes = slice(side * 128, side * 128 + 128)
+                    rows_ref[rows, :] = rows_ref[rows, :] + force[y * 64 : y * 64 + 64, lanes]
+        for side in range(2):
+            grid_out(step, side, True).start()
+        return carry
+
+    lax.fori_loop(0, steps, body, 0)
+    for step in range(steps):
+        for side in range(2):
+            grid_out(step, side, True).wait()
 
 
 def params(count):
@@ -425,21 +495,36 @@
 def call_z_forward(phi, table):
     return pl.pallas_call(
         z_forward,
-        grid=(2, groups),
-        in_specs=[
-            pl.BlockSpec((2, 32, 16, 128), lambda j, g: (g, 0, j, 0)),
-            pl.BlockSpec((2, 32, 16, 128), lambda j, g: (g, 0, j, 1)),
-            whole(table),
+        in_specs=[whole(table), anywhere],
+        out_specs=[anywhere, anywhere],
+        out_shape=[hbm((128, 2 * groups, 16, 128)), hbm((32, 32, 256))],
+        scratch_shapes=[
+            pltpu.VMEM((2 * groups, 2, 2, 32, 24, 128), jnp.float32),
+            pltpu.VMEM((2 * groups, 128, 3, 8, 128), jnp.float32),
+            pltpu.VMEM((32, 32, 256), jnp.float32),
+            pltpu.SemaphoreType.DMA((5, 2 * groups)),
         ],
-        out_specs=[
-            pl.BlockSpec((128, 2, 8, 128), lambda j, g: (0, g, j, 0)),
-            pl.BlockSpec((32, 16, 256), lambda j, g: (0, j, 0)),
-        ],
-        out_shape=[hbm((128, 2 * groups, 16, 128)), hbm((32, 32, 256))],
-        compiler_params=params(2),
+        compiler_params=pltpu.CompilerParams(vmem_limit_bytes=vmem_bytes),
         cost_estimate=cost(2.4e9, 2 * groups * group_bytes),
         name="z_forward",
-    )(phi, phi, table)
+    )(table, phi)
+
+
+def call_local(phi, own, partner):
+    return pl.pallas_call(
+        local_part,
+        grid=(groups, 4),
+        in_specs=[
+            pl.BlockSpec((2, 32, 8, 256), lambda g, j: (g, 0, j, 0)),
+            pl.BlockSpec((32, 8, 256), lambda g, j: (0, j, 0)),
+            pl.BlockSpec((32, 8, 256), lambda g, j: (0, j, 0)),
+        ],
+        out_specs=pl.BlockSpec((2, 32, 8, 256), lambda g, j: (g, 0, j, 0)),
+        out_shape=hbm(phi.shape),
+        compiler_params=params(2),
+        cost_estimate=cost(50e6, 3 * groups * group_bytes),
+        name="local_part",
+    )(phi, in_hbm(own), in_hbm(partner))
 
 
 smem = pl.BlockSpec(memory_space=pltpu.SMEM)
@@ -467,24 +552,21 @@
     )(coefs, spec, *tables)
 
 
-def call_z_back(spec, phi, own, partner, table):
+def call_z_back(spec, base, table):
     return pl.pallas_call(
         z_back,
-        grid=(2, groups),
-        in_specs=[
-            pl.BlockSpec((128, 2, 8, 128), lambda j, g: (0, g, j, 0)),
-            pl.BlockSpec((2, 32, 16, 256), lambda j, g: (g, 0, j, 0)),
-            pl.BlockSpec((32, 16, 256), lambda j, g: (0, j, 0)),
-            pl.BlockSpec((32, 16, 256), lambda j, g: (0, j, 0)),
-            whole(table),
+        in_specs=[whole(table), anywhere, anywhere],
+        out_specs=anywhere,
+        out_shape=hbm(base.shape),
+        scratch_shapes=[
+            pltpu.VMEM((2 * groups, 128, 3, 8, 128), jnp.float32),
+            pltpu.VMEM((2 * groups, 2, 2, 32, 24, 128), jnp.float32),
+            pltpu.SemaphoreType.DMA((5, 2 * groups)),
         ],
-        out_specs=pl.BlockSpec((2, 32, 16, 256), lambda j, g: (g, 0, j, 0)),
-        out_shape=hbm(phi.shape),
-        scratch_shapes=[pltpu.VMEM((2, 2, 32, 16, 128), jnp.float32)],
-        compiler_params=params(2),
+        compiler_params=pltpu.CompilerParams(vmem_limit_bytes=vmem_bytes),
         cost_estimate=cost(2.4e9, 3 * groups * group_bytes),
         name="z_back",
-    )(spec, phi, in_hbm(own), in_hbm(partner), table)
+    )(table, spec, in_hbm(base))
 
 
 def exchange(block):
@@ -518,7 +600,8 @@
     sent = call_middle(coefs, arrived, (y_fwd, x_fwd, x_inv, y_inv))
     sent, partner = lax.optimization_barrier((sent, partner))
     returned = exchange(sent)
-    return call_z_back(returned, order_field, squares, partner, z_inv)
+    base = call_local(order_field, squares, partner)
+    return call_z_back(returned, base, z_inv)
 
 
 def solution(mesh):

time: 234 us -> 216 us (0.923)
  blocking collectives: 90.1 us -> 0 us
  waiting for transfers between devices: 80.5 us -> 135 us
  starting transfers between devices: 11.9 us -> 22.3 us
  Pallas kernels: 50.4 us -> 56.8 us
    all_to_all x1 -> x0, blocking collectives: 90.1 us -> none  [exchange(): return lax.all_to_all(block, every, split_axis=0, concat_axis=0, tiled=True)]
    all_to_all x1 -> x2, waiting for transfers between devices: 80.5 us -> 135 us  [exchange(): return lax.all_to_all(block, every, split_axis=0, concat_axis=0, tiled=True)]
    all_to_all x1 -> x2, starting transfers between devices: 11.9 us -> 21.9 us  [exchange(): return lax.all_to_all(block, every, split_axis=0, concat_axis=0, tiled=True)]
    pallas_call x2 -> x3, Pallas kernels: 22.6 us -> 29 us  [the longest x1 11.2 us: call_local(): pl.pallas_call(local_part, grid=(groups, 4), in_specs=[pl.BlockSpec((2, 3...]
  transfers between devices with their start and end apart: 2 -> 3, of which waited for: 1 -> 2; matrix products, arithmetic and copies ran while one was open for 0% -> 0% of each run, Pallas kernels for 12% -> 18%
where the time goes in v3:
time: 216 us; the launch traced here: 215 us
  waiting for transfers between devices  135 us (62%)
  Pallas kernels  56.8 us (26%)
  starting transfers between devices  22.3 us (10%)
    all_to_all x2, waiting for transfers between devices, exchange(): return lax.all_to_all(block, every, split_axis=0, concat_axis=0, tiled=True)  135 us
    pallas_call x1, Pallas kernels, call_middle(): pl.pallas_call(middle, in_specs=[smem] + [anywhere] * (1 + len(tables)),...  27.8 us
    all_to_all x2, starting transfers between devices, exchange(): return lax.all_to_all(block, every, split_axis=0, concat_axis=0, tiled=True)  21.9 us
    pallas_call x1, Pallas kernels, call_local(): pl.pallas_call(local_part, grid=(groups, 4), in_specs=[pl.BlockSpec((2, 3...  11.2 us
    pallas_call x1, Pallas kernels, call_z_back(): pl.pallas_call(z_back, in_specs=[whole(table), anywhere, anywhere], out_s...  9.02 us
    pallas_call x1, Pallas kernels, call_z_forward(): pl.pallas_call(z_forward, in_specs=[whole(table), anywhere], out_specs=[a...  8.7 us
  transfers between devices with their start and end apart: 3, of which 2 were waited for; matrix products, arithmetic and copies ran while one was open for 0% of the time, Pallas kernels for 18%

profile of v3, /device:TPU:1, one launch (start us, length us, event | category | flops | bytes accessed | tf_op | source)
XLA Modules:
  0.0 215.0 jit_solution(1043868980051899124)
XLA Ops:
  0.0 0.0 copy-start
  0.0 8.7 %z_forward.1 = (f32[128,6,16,128]{3,2,1,0:T(8,128)}, f32[32,32,256]{2,1,0:T(8,128)}) custom-call(bf16[256,512]{1,0:T(8,128)(2,1)} %constant.35.clone.table_ref, f32[6,32,32,256]{3,2,1,0:T(8,128)} %phi_ref.1), custom_call_target="tpu_custom_call" | custom-call | flops 2400000000 | bytes 12582912 | tf_op jit(solution)/shard_map/z_forward/pallas_call | solution.py:496
  8.7 0.0 copy-start.4
  8.7 0.0 copy-start.3
  8.7 0.0 copy-start.1
  8.7 11.9 %all-to-all-start = ((f32[128,6,16,128]{3,2,1,0:T(8,128)}), f32[128,6,16,128]{3,2,1,0:T(8,128)}, u32[]{:S(2)}, u32[]{:S(2)}) async-start(f32[128,6,16,128]{3,2,1,0:T(8,128)} %get-tuple-element.12), calls=%async_computation | async-start | bytes 12582912 | tf_op jit(solution)/shard_map/all_to_all | solution.py:573
  20.7 0.0 copy-done
  20.7 0.0 copy-done.4
  20.7 0.2 fusion
  20.9 0.1 copy.15
  21.0 0.0 copy-done.3
  21.0 0.1 multiply_add_fusion
  21.1 0.1 select_maximum_fusion.coef_ref
  21.1 73.0 %all-to-all-done.in_hbm = f32[128,6,16,128]{3,2,1,0:T(8,128)} async-done(((f32[128,6,16,128]{3,2,1,0:T(8,128)}), f32[128,6,16,128]{3,2,1,0:T(8,128)}, u32[]{:S(2)}, u32[]{:S(2)}) %all-to-all-start) | async-done | bytes 6291488 | tf_op jit(solution)/shard_map/all_to_all | solution.py:573
  94.2 0.0 copy-done.1
  94.2 0.5 collective-permute-start
  94.6 27.8 %middle.1 = f32[128,6,16,128]{3,2,1,0:T(8,128)} custom-call(f32[13,12]{1,0:T(8,128)S(1)} %select_maximum_fusion.coef_ref, f32[128,6,16,128]{3,2,1,0:T(8,128)} %all-to-all-done.in_hbm, bf16[2,256,512]{2,1,0:T(8,128)(2,1)} %constant.37.clone.yf_hbm, bf16[2,512,256]{2,1,0:T(8,128)(2,1)} %constant.39.clone.xf_hbm, bf16[2,512,256]{2,1,0:T(8,128)(2,1)} %constant.40.clone.xb_hbm, ...), custom_call_target="tpu_custom_call" | custom-call | flops 20000000000 | bytes 37748736 | tf_op jit(solution)/shard_map/middle/pallas_call | solution.py:543
  122.4 0.0 collective-permute-done.partner_ref
  122.5 0.0 copy-start.2
  122.5 10.0 %all-to-all-start.1 = ((f32[128,6,16,128]{3,2,1,0:T(8,128)}), f32[128,6,16,128]{3,2,1,0:T(8,128)}, u32[]{:S(2)}, u32[]{:S(2)}) async-start(f32[128,6,16,128]{3,2,1,0:T(8,128)} %middle.1), calls=%async_computation.1 | async-start | bytes 12582912 | tf_op jit(solution)/shard_map/all_to_all | solution.py:573
  132.5 0.0 copy-done.2
  132.5 11.2 %local_part.1.base_hbm = f32[6,32,32,256]{3,2,1,0:T(8,128)} custom-call(f32[6,32,32,256]{3,2,1,0:T(8,128)} %phi_ref.1, f32[32,32,256]{2,1,0:T(8,128)} %get-tuple-element.14.own_ref, f32[32,32,256]{2,1,0:T(8,128)} %copy-done.2), custom_call_target="tpu_custom_call" | custom-call | flops 50000000 | bytes 18874368 | tf_op jit(solution)/shard_map/local_part/pallas_call | solution.py:514
  143.7 62.3 %all-to-all-done.1.spec_hbm = f32[128,6,16,128]{3,2,1,0:T(8,128)} async-done(((f32[128,6,16,128]{3,2,1,0:T(8,128)}), f32[128,6,16,128]{3,2,1,0:T(8,128)}, u32[]{:S(2)}, u32[]{:S(2)}) %all-to-all-start.1) | async-done | bytes 6291488 | tf_op jit(solution)/shard_map/all_to_all | solution.py:573
  206.0 9.0 %z_back.1 = f32[6,32,32,256]{3,2,1,0:T(8,128)} custom-call(bf16[512,256]{1,0:T(8,128)(2,1)} %constant.36.clone.table_ref, f32[128,6,16,128]{3,2,1,0:T(8,128)} %all-to-all-done.1.spec_hbm, f32[6,32,32,256]{3,2,1,0:T(8,128)} %local_part.1.base_hbm), custom_call_target="tpu_custom_call" | custom-call | flops 2400000000 | bytes 18874368 | tf_op jit(solution)/shard_map/z_back/pallas_call | solution.py:556
  (1 shorter events, 0.0 us)
Async XLA Ops:
  0.0 20.7 %copy-start = (f32[24,6]{0,1:T(8,128)S(1)}, f32[24,6]{0,1:T(8,128)}, u32[]{:S(2)}) copy-start(f32[24,6]{0,1:T(8,128)} %param.11) | copy-start | bytes 1732
  8.7 12.0 %copy-start.4 = (s32[24]{0:T(128)S(1)}, s32[24]{0:T(128)}, u32[]{:S(2)}) copy-start(s32[24]{0:T(128)} %param.12) | copy-start | bytes 292
  8.7 12.3 %copy-start.3 = (f32[6]{0:T(128)S(1)}, f32[6]{0:T(128)}, u32[]{:S(2)}) copy-start(f32[6]{0:T(128)} %constant.41.clone) | copy-start | bytes 76
  8.7 85.4 %copy-start.1 = (f32[32,32,256]{2,1,0:T(8,128)S(1)}, f32[32,32,256]{2,1,0:T(8,128)}, u32[]{:S(2)}) copy-start(f32[32,32,256]{2,1,0:T(8,128)} %get-tuple-element.14.own_ref) | copy-start | bytes 3145732
  8.7 85.4 %all-to-all-start = ((f32[128,6,16,128]{3,2,1,0:T(8,128)}), f32[128,6,16,128]{3,2,1,0:T(8,128)}, u32[]{:S(2)}, u32[]{:S(2)}) async-start(f32[128,6,16,128]{3,2,1,0:T(8,128)} %get-tuple-element.12), calls=%async_computation | async-start | bytes 12582912 | tf_op jit(solution)/shard_map/all_to_all | solution.py:573
  94.2 28.3 %collective-permute-start = (f32[32,32,256]{2,1,0:T(8,128)S(1)}, f32[32,32,256]{2,1,0:T(8,128)S(1)}, u32[]{:S(2)}, u32[]{:S(2)}) collective-permute-start(f32[32,32,256]{2,1,0:T(8,128)S(1)} %copy-done.1), channel_id=1, source_target_pairs={{0,64},{64,0},{1,65},{65,1},{2,66},{66,2},{3,67},{67,3},{4,68},{68... | collective-permute-start | bytes 3145736 | tf_op jit(solution)/shard_map/ppermute | solution.py:599
  122.5 10.0 %copy-start.2 = (f32[32,32,256]{2,1,0:T(8,128)}, f32[32,32,256]{2,1,0:T(8,128)S(1)}, u32[]{:S(2)}) copy-start(f32[32,32,256]{2,1,0:T(8,128)S(1)} %collective-permute-done.partner_ref) | copy-start | bytes 3145732
  122.5 83.5 %all-to-all-start.1 = ((f32[128,6,16,128]{3,2,1,0:T(8,128)}), f32[128,6,16,128]{3,2,1,0:T(8,128)}, u32[]{:S(2)}, u32[]{:S(2)}) async-start(f32[128,6,16,128]{3,2,1,0:T(8,128)} %middle.1), calls=%async_computation.1 | async-start | bytes 12582912 | tf_op jit(solution)/shard_map/all_to_all | solution.py:573

commit v4 on v3

--- a/solution.py
+++ b/solution.py
@@ -19,7 +19,7 @@
 two_pi = 6.283185307179586
 highest = lax.Precision.HIGHEST
 every = ("var", "pz", "py")
-vmem_bytes = 48 * 1024 * 1024
+vmem_bytes = 36 * 1024 * 1024
 
 groups = 3
 
@@ -144,12 +144,15 @@
     return spec, grid
 
 
-def z_forward(table_ref, phi_hbm, out_hbm, sq_hbm, phi_ref, out_ref, sq_ref, sems):
+def z_forward(table_hbm, phi_hbm, out_hbm, sq_hbm, table_ref, phi_ref, out_ref, sq_ref, sems):
     spec, grid = z_pieces(out_hbm, out_ref, phi_hbm, phi_ref, sems)
     steps = groups * 2
+    table = pltpu.make_async_copy(table_hbm, table_ref, sems.at[4, 0])
+    table.start()
     for step in range(steps):
         for side in range(2):
             grid(step, side, False).start()
+    table.wait()
     sq_ref[...] = jnp.zeros_like(sq_ref)
     rows_ref = phi_ref.reshape(steps * 3072, 128)
     flat_ref = out_ref.reshape(steps * 3072, 128)
@@ -196,7 +199,7 @@
     last.wait()
 
 
-def transform_there(in_ref, y_ref, x_ref, out_ref, left_ref):
+def y_there(in_ref, y_ref, left_ref):
     lanes = lane_ids(256)
     low_half = lanes < 64
     first_bit = lane_ids(128) // 32 % 2 == 0
@@ -234,30 +237,37 @@
                 for v, value in enumerate(values):
                     high, low = split_value(value)
                     start = v * 256 + side * 128
-                    for third, piece in enumerate((high, low, high)):
-                        column = third * 256 + part * 128
+                    for place, piece in enumerate((high, low)):
+                        column = place * 256 + part * 128
                         left_ref[parity, start : start + 128, column : column + 128] = piece
+
+
+def x_there(left_ref, x_ref, out_ref):
     for parity in range(2):
-        product = matmul(left_ref[parity], right_rows(x_ref[parity]))
+        product = matmul(left_rows(left_ref[parity]), right_rows(x_ref[parity]))
         for v in range(2):
             out_ref[v, :, parity * 256 : parity * 256 + 256] = product[v * 256 : v * 256 + 256]
 
 
-def transform_back(in_ref, x_ref, y_ref, out_ref):
-    lanes = lane_ids(256)
-    low_half = lanes < 64
-    first_bit = lanes // 32 % 2 == 0
+def x_back(in_ref, x_ref, mid_ref):
     products = []
     for parity in range(2):
         columns = slice(parity * 256, parity * 256 + 256)
         block = jnp.concatenate([in_ref[0, :, columns], in_ref[1, :, columns]], axis=0)
         products.append(matmul(as_left(block), right_rows(x_ref[parity])))
+    mid_ref[0] = products[0] + products[1]
+    mid_ref[1] = products[0] - products[1]
+
+
+def y_back(mid_ref, y_ref, out_ref):
+    lanes = lane_ids(256)
+    low_half = lanes < 64
+    first_bit = lanes // 32 % 2 == 0
     for side in range(2):
-        field = products[0] + products[1] if side == 0 else products[0] - products[1]
         evens, odds = ([], []), ([], [])
         for part in range(2):
-            zero = field[:256, part * 128 : part * 128 + 128]
-            one = field[256:, part * 128 : part * 128 + 128]
+            zero = mid_ref[side, :256, part * 128 : part * 128 + 128]
+            one = mid_ref[side, 256:, part * 128 : part * 128 + 128]
             merged = (
                 jnp.where(first_bit, zero, pltpu.roll(one, 32, 1)),
                 jnp.where(first_bit, pltpu.roll(zero, 96, 1), one),
@@ -281,19 +291,23 @@
                 out_ref[pz * 8 + place + 1] = second[rows].reshape(2, 16, 128)
 
 
-def waves(row, wave_z, length):
+def signed_index(indices, length):
     half = length // 2
+    return jnp.where(indices >= half, indices - length, indices).astype(jnp.float32)
+
+
+def waves_x(wave_z, length):
+    half = length // 2
+    column = lax.broadcasted_iota(jnp.int32, (8, length), 1)
+    kx = jnp.where(column >= half, column * 2 - (length - 1), column * 2)
+    wx = signed_index(kx, length)
+    keep = jnp.where(kx == half, 0.0, 1.0 / float(length * length * length))
+    return wx, wx * wx + wave_z * wave_z, keep
+
+
+def waves_y(row, length):
     ky = lax.broadcasted_iota(jnp.int32, (8, length), 0) + row
-    column = lax.broadcasted_iota(jnp.int32, (8, length), 1)
-    kx = column % half * 2 + column // half
-    wy = jnp.where(ky >= half, ky - length, ky).astype(jnp.float32)
-    wx = jnp.where(kx >= half, kx - length, kx).astype(jnp.float32)
-    wz = jnp.full((8, length), wave_z, jnp.float32)
-    squared = wx * wx + wy * wy + wz * wz
-    volume = 1.0 / float(length * length * length)
-    keep = jnp.where((ky == half) | (kx == half), 0.0, volume)
-    grad = keep * squared * (grad_coef * (two_pi / length) ** 2)
-    return wx, wy, wz, squared, keep, join(grad, grad)
+    return signed_index(ky, length), jnp.where(ky == length // 2, 0.0, 1.0)
 
 
 def pick(value, part):
@@ -335,10 +349,9 @@
     ]
 
 
-def middle(coef_ref, in_hbm, yf_hbm, xf_hbm, xb_hbm, yb_hbm, out_hbm, *scratch):
-    in_ref, yf_ref, xf_ref, xb_ref, yb_ref, field_ref, left_ref, out_ref, sems = scratch
+def middle(coef_hbm, in_ref, yf_hbm, xf_hbm, xb_hbm, yb_hbm, out_hbm, *scratch):
+    yf_ref, xf_ref, xb_ref, yb_ref, coef_ref, field_ref, lefts, mids, out_ref, sems = scratch
     length = field_ref.shape[1]
-    wave_z = coef_ref[12, 0]
     steps = groups * 2
 
     def part_of(ref, step):
@@ -347,51 +360,62 @@
             pl.ds(pl.multiple_of(step // 2 * 2, 2), 2),
         ]
 
-    def arrival(step):
-        slot = step % 2
-        return pltpu.make_async_copy(part_of(in_hbm, step), in_ref.at[slot], sems.at[slot])
-
     def departure(step):
-        slot = step % 2
-        return pltpu.make_async_copy(out_ref.at[slot], part_of(out_hbm, step), sems.at[2 + slot])
+        return pltpu.make_async_copy(out_ref.at[step], part_of(out_hbm, step), sems.at[1, step])
+
+    def fields_of(step):
+        return field_ref.at[pl.ds(step * 2, 2)]
 
     moves = [(yf_hbm, yf_ref), (xf_hbm, xf_ref), (xb_hbm, xb_ref), (yb_hbm, yb_ref)]
+    moves.append((coef_hbm, coef_ref))
     copies = [
-        pltpu.make_async_copy(source, target, sems.at[4 + number])
+        pltpu.make_async_copy(source, target, sems.at[0, number])
         for number, (source, target) in enumerate(moves)
     ]
-    copies[0].start()
-    arrival(0).start()
-    for copy in copies[1:]:
+    for copy in copies:
         copy.start()
+
+    def there_first(step, slot):
+        y_there(part_of(in_ref, step), yf_ref, lefts[slot])
+
+    def there_second(step, slot):
+        x_there(lefts[slot], xf_ref, fields_of(step))
+
     copies[0].wait()
+    there_first(0, 0)
     copies[1].wait()
 
-    def there(step, carry):
-        @pl.when(step + 1 < steps)
-        def _():
-            arrival(step + 1).start()
-
-        arrival(step).wait()
-        transform_there(
-            in_ref.at[step % 2], yf_ref, xf_ref, field_ref.at[pl.ds(step * 2, 2)], left_ref
-        )
+    def there(turn, carry):
+        for slot in range(2):
+            there_first(turn * 2 + slot + 1, 1 - slot)
+            there_second(turn * 2 + slot, slot)
         return carry
 
-    lax.fori_loop(0, steps, there, 0)
+    lax.fori_loop(0, groups - 1, there, 0)
+    there_first(steps - 1, 1)
+    there_second(steps - 2, 0)
+    there_second(steps - 1, 1)
+    copies[4].wait()
+    wave_z = coef_ref[12, 0]
     places = [(p % 6 // 2 * 2 + p // 6) * 2 + p % 2 for p in range(12)]
+
+    wx, squared_xz, keep_x = waves_x(wave_z, length)
 
     def tile(step, carry):
         row = pl.multiple_of(step * 8, 8)
         rows = pl.ds(row, 8)
-        wx, wy, wz, squared, keep, grad = waves(row, wave_z, length)
+        wy, keep_y = waves_y(row, length)
+        squared = squared_xz + wy * wy
+        keep = keep_x * keep_y
+        half_grad = keep * squared * (grad_coef * (two_pi / length) ** 2)
+        grad = join(half_grad, half_grad)
         strains = None
         for q, place in enumerate(places):
             value = field_ref[place, rows, :]
             terms = [coef_ref[q, m] * value for m in range(6)]
             strains = terms if q == 0 else [total + term for total, term in zip(strains, terms)]
         parts = [
-            driving([pick(total, part) for total in strains], wx, wy, wz, squared, keep)
+            driving([pick(total, part) for total in strains], wx, wy, wave_z, squared, keep)
             for part in range(2)
         ]
         drive = [join(parts[0][m], parts[1][m]) for m in range(6)]
@@ -406,18 +430,27 @@
     copies[2].wait()
     copies[3].wait()
 
-    def back(step, carry):
-        @pl.when(step >= 2)
-        def _():
-            departure(step - 2).wait()
-
-        transform_back(field_ref.at[pl.ds(step * 2, 2)], xb_ref, yb_ref, out_ref.at[step % 2])
+    def back_first(step, slot):
+        x_back(fields_of(step), xb_ref, mids[slot])
+
+    def back_second(step, slot):
+        y_back(mids[slot], yb_ref, out_ref.at[step])
         departure(step).start()
+
+    back_first(0, 0)
+
+    def back(turn, carry):
+        for slot in range(2):
+            back_first(turn * 2 + slot + 1, 1 - slot)
+            back_second(turn * 2 + slot, slot)
         return carry
 
-    lax.fori_loop(0, steps, back, 0)
-    departure(steps - 2).wait()
-    departure(steps - 1).wait()
+    lax.fori_loop(0, groups - 1, back, 0)
+    back_first(steps - 1, 1)
+    back_second(steps - 2, 0)
+    back_second(steps - 1, 1)
+    for step in range(steps):
+        departure(step).wait()
 
 
 def local_part(phi_ref, own_ref, partner_ref, out_ref):
@@ -427,14 +460,18 @@
     out_ref[...] = phi - mobility * chemical
 
 
-def z_back(table_ref, spec_hbm, base_hbm, out_hbm, spec_ref, base_ref, sems):
+def z_back(table_hbm, spec_hbm, base_hbm, out_hbm, table_ref, spec_ref, base_ref, sems):
     spec, grid = z_pieces(spec_hbm, spec_ref, base_hbm, base_ref, sems)
     grid_out = z_pieces(spec_hbm, spec_ref, out_hbm, base_ref, sems)[1]
     steps = groups * 2
+    table = pltpu.make_async_copy(table_hbm, table_ref, sems.at[5, 0])
     for step in range(steps):
         spec(step, False).start()
         for side in range(2):
             grid(step, side, False).start()
+        if step == 0:
+            table.start()
+    table.wait()
     flat_ref = spec_ref.reshape(steps * 3072, 128)
     rows_ref = base_ref.reshape(steps * 3072, 128)
 
@@ -485,20 +522,17 @@
     return pltpu.with_memory_space_constraint(array, pltpu.HBM)
 
 
-def whole(array):
-    return pl.BlockSpec(array.shape, lambda *ids: (0,) * array.ndim)
-
-
 group_bytes = 2 * 32 * 32 * 256 * 4
 
 
 def call_z_forward(phi, table):
     return pl.pallas_call(
         z_forward,
-        in_specs=[whole(table), anywhere],
+        in_specs=[anywhere, anywhere],
         out_specs=[anywhere, anywhere],
         out_shape=[hbm((128, 2 * groups, 16, 128)), hbm((32, 32, 256))],
         scratch_shapes=[
+            pltpu.VMEM(table.shape, jnp.bfloat16),
             pltpu.VMEM((2 * groups, 2, 2, 32, 24, 128), jnp.float32),
             pltpu.VMEM((2 * groups, 128, 3, 8, 128), jnp.float32),
             pltpu.VMEM((32, 32, 256), jnp.float32),
@@ -507,7 +541,7 @@
         compiler_params=pltpu.CompilerParams(vmem_limit_bytes=vmem_bytes),
         cost_estimate=cost(2.4e9, 2 * groups * group_bytes),
         name="z_forward",
-    )(table, phi)
+    )(table, in_hbm(phi))
 
 
 def call_local(phi, own, partner):
@@ -524,44 +558,46 @@
         compiler_params=params(2),
         cost_estimate=cost(50e6, 3 * groups * group_bytes),
         name="local_part",
-    )(phi, in_hbm(own), in_hbm(partner))
-
-
-smem = pl.BlockSpec(memory_space=pltpu.SMEM)
+    )(in_hbm(phi), in_hbm(own), in_hbm(partner))
+
+
 anywhere = pl.BlockSpec(memory_space=pl.ANY)
+inside = pl.BlockSpec(memory_space=pltpu.VMEM)
 
 
 def call_middle(coefs, spec, tables):
     shapes = [
-        pltpu.VMEM((2, 64, 2, 16, 128), jnp.float32),
         *[pltpu.VMEM(table.shape, jnp.bfloat16) for table in tables],
+        pltpu.SMEM(coefs.shape, jnp.float32),
         pltpu.VMEM((4 * groups, 256, 512), jnp.float32),
-        pltpu.VMEM((2, 512, 768), jnp.bfloat16),
-        pltpu.VMEM((2, 64, 2, 16, 128), jnp.float32),
-        pltpu.SemaphoreType.DMA((8,)),
+        [pltpu.VMEM((2, 512, 512), jnp.bfloat16)] * 2,
+        [pltpu.VMEM((2, 512, 256), jnp.float32)] * 2,
+        pltpu.VMEM((2 * groups, 64, 2, 16, 128), jnp.float32),
+        pltpu.SemaphoreType.DMA((2, 2 * groups)),
     ]
     return pl.pallas_call(
         middle,
-        in_specs=[smem] + [anywhere] * (1 + len(tables)),
+        in_specs=[anywhere, inside] + [anywhere] * len(tables),
         out_specs=anywhere,
         out_shape=hbm(spec.shape),
         scratch_shapes=shapes,
         compiler_params=pltpu.CompilerParams(vmem_limit_bytes=vmem_bytes),
         cost_estimate=cost(20e9, 6 * groups * group_bytes),
         name="middle",
-    )(coefs, spec, *tables)
+    )(coefs, pltpu.with_memory_space_constraint(spec, pltpu.VMEM), *tables)
 
 
 def call_z_back(spec, base, table):
     return pl.pallas_call(
         z_back,
-        in_specs=[whole(table), anywhere, anywhere],
+        in_specs=[anywhere, anywhere, anywhere],
         out_specs=anywhere,
         out_shape=hbm(base.shape),
         scratch_shapes=[
+            pltpu.VMEM(table.shape, jnp.bfloat16),
             pltpu.VMEM((2 * groups, 128, 3, 8, 128), jnp.float32),
             pltpu.VMEM((2 * groups, 2, 2, 32, 24, 128), jnp.float32),
-            pltpu.SemaphoreType.DMA((5, 2 * groups)),
+            pltpu.SemaphoreType.DMA((6, 2 * groups)),
         ],
         compiler_params=pltpu.CompilerParams(vmem_limit_bytes=vmem_bytes),
         cost_estimate=cost(2.4e9, 3 * groups * group_bytes),

time: 216 us -> 212 us (0.981)
  Pallas kernels: 56.8 us -> 52.9 us
    pallas_call x3, Pallas kernels: 45.5 us -> 41.7 us  [the longest x1 25.7 us: call_middle(): pl.pallas_call(middle, in_specs=[anywhere, inside] + [anywhere] * len(tab...]
  transfers between devices with their start and end apart: 3 -> 3, of which waited for: 2 -> 2; matrix products, arithmetic and copies ran while one was open for 0% -> 0% of each run, Pallas kernels for 18% -> 17%
where the time goes in v4:
time: 212 us; the launch traced here: 211 us
  waiting for transfers between devices  135 us (64%)
  Pallas kernels  52.9 us (25%)
  starting transfers between devices  22.3 us (11%)
    all_to_all x2, waiting for transfers between devices, exchange(): return lax.all_to_all(block, every, split_axis=0, concat_axis=0, tiled=True)  135 us
    pallas_call x1, Pallas kernels, call_middle(): pl.pallas_call(middle, in_specs=[anywhere, inside] + [anywhere] * len(tab...  25.7 us
    all_to_all x2, starting transfers between devices, exchange(): return lax.all_to_all(block, every, split_axis=0, concat_axis=0, tiled=True)  21.9 us
    pallas_call x1, Pallas kernels, call_local(): pl.pallas_call(local_part, grid=(groups, 4), in_specs=[pl.BlockSpec((2, 3...  11.2 us
    pallas_call x1, Pallas kernels, call_z_back(): pl.pallas_call(z_back, in_specs=[anywhere, anywhere, anywhere], out_specs...  8.16 us
    pallas_call x1, Pallas kernels, call_z_forward(): pl.pallas_call(z_forward, in_specs=[anywhere, anywhere], out_specs=[anywh...  7.83 us
  transfers between devices with their start and end apart: 3, of which 2 were waited for; matrix products, arithmetic and copies ran while one was open for 0% of the time, Pallas kernels for 17%

profile of v4, /device:TPU:1, one launch (start us, length us, event | category | flops | bytes accessed | tf_op | source)
XLA Modules:
  0.0 211.1 jit_solution(1178779788827510750)
XLA Ops:
  0.0 0.0 copy-start
  0.0 7.8 %z_forward.1 = (f32[128,6,16,128]{3,2,1,0:T(8,128)}, f32[32,32,256]{2,1,0:T(8,128)}) custom-call(bf16[256,512]{1,0:T(8,128)(2,1)} %constant.35.clone.table_hbm, f32[6,32,32,256]{3,2,1,0:T(8,128)} %phi_ref.1), custom_call_target="tpu_custom_call" | custom-call | flops 2400000000 | bytes 12582912 | tf_op jit(solution)/shard_map/z_forward/pallas_call | solution.py:529
  7.8 0.0 copy-start.4
  7.9 0.0 copy-start.3
  7.9 0.0 copy-start.1
  7.9 11.9 %all-to-all-start = ((f32[128,6,16,128]{3,2,1,0:T(8,128)}), f32[128,6,16,128]{3,2,1,0:T(8,128)}, u32[]{:S(2)}, u32[]{:S(2)}) async-start(f32[128,6,16,128]{3,2,1,0:T(8,128)} %get-tuple-element.12), calls=%async_computation | async-start | bytes 12582912 | tf_op jit(solution)/shard_map/all_to_all | solution.py:609
  19.8 0.0 copy-done
  19.8 0.0 copy-done.4
  19.8 0.2 fusion
  20.0 0.1 copy.15
  20.1 0.0 copy-done.3
  20.1 0.1 multiply_add_fusion
  20.2 0.1 select_maximum_fusion.coef_hbm
  20.3 73.0 %all-to-all-done.in_ref = f32[128,6,16,128]{3,2,1,0:T(8,128)} async-done(((f32[128,6,16,128]{3,2,1,0:T(8,128)}), f32[128,6,16,128]{3,2,1,0:T(8,128)}, u32[]{:S(2)}, u32[]{:S(2)}) %all-to-all-start) | async-done | bytes 6291488 | tf_op jit(solution)/shard_map/all_to_all | solution.py:609
  93.3 0.0 copy-done.1
  93.3 0.5 collective-permute-start
  93.8 25.7 %middle.1 = f32[128,6,16,128]{3,2,1,0:T(8,128)} custom-call(f32[13,12]{1,0:T(8,128)S(1)} %select_maximum_fusion.coef_hbm, f32[128,6,16,128]{3,2,1,0:T(8,128)} %all-to-all-done.in_ref, bf16[2,256,512]{2,1,0:T(8,128)(2,1)} %constant.37.clone.yf_hbm, bf16[2,512,256]{2,1,0:T(8,128)(2,1)} %constant.39.clone.xf_hbm, bf16[2,512,256]{2,1,0:T(8,128)(2,1)} %constant.40.clone.xb_hbm, ...), custom_call_target="tpu_custom_call" | custom-call | flops 20000000000 | bytes 37748736 | tf_op jit(solution)/shard_map/middle/pallas_call | solution.py:578
  119.4 0.0 collective-permute-done.partner_ref
  119.4 0.0 copy-start.2
  119.4 10.0 %all-to-all-start.1 = ((f32[128,6,16,128]{3,2,1,0:T(8,128)}), f32[128,6,16,128]{3,2,1,0:T(8,128)}, u32[]{:S(2)}, u32[]{:S(2)}) async-start(f32[128,6,16,128]{3,2,1,0:T(8,128)} %middle.1), calls=%async_computation.1 | async-start | bytes 12582912 | tf_op jit(solution)/shard_map/all_to_all | solution.py:609
  129.4 0.0 copy-done.2
  129.4 11.2 %local_part.1.base_hbm = f32[6,32,32,256]{3,2,1,0:T(8,128)} custom-call(f32[6,32,32,256]{3,2,1,0:T(8,128)} %phi_ref.1, f32[32,32,256]{2,1,0:T(8,128)} %get-tuple-element.14.own_ref, f32[32,32,256]{2,1,0:T(8,128)} %copy-done.2), custom_call_target="tpu_custom_call" | custom-call | flops 50000000 | bytes 18874368 | tf_op jit(solution)/shard_map/local_part/pallas_call | solution.py:548
  140.7 62.3 %all-to-all-done.1.spec_hbm = f32[128,6,16,128]{3,2,1,0:T(8,128)} async-done(((f32[128,6,16,128]{3,2,1,0:T(8,128)}), f32[128,6,16,128]{3,2,1,0:T(8,128)}, u32[]{:S(2)}, u32[]{:S(2)}) %all-to-all-start.1) | async-done | bytes 6291488 | tf_op jit(solution)/shard_map/all_to_all | solution.py:609
  202.9 8.2 %z_back.1 = f32[6,32,32,256]{3,2,1,0:T(8,128)} custom-call(bf16[512,256]{1,0:T(8,128)(2,1)} %constant.36.clone.table_hbm, f32[128,6,16,128]{3,2,1,0:T(8,128)} %all-to-all-done.1.spec_hbm, f32[6,32,32,256]{3,2,1,0:T(8,128)} %local_part.1.base_hbm), custom_call_target="tpu_custom_call" | custom-call | flops 2400000000 | bytes 18874368 | tf_op jit(solution)/shard_map/z_back/pallas_call | solution.py:591
  (1 shorter events, 0.0 us)
Async XLA Ops:
  0.0 19.8 %copy-start = (f32[24,6]{0,1:T(8,128)S(1)}, f32[24,6]{0,1:T(8,128)}, u32[]{:S(2)}) copy-start(f32[24,6]{0,1:T(8,128)} %param.11) | copy-start | bytes 1732
  7.8 12.0 %copy-start.4 = (s32[24]{0:T(128)S(1)}, s32[24]{0:T(128)}, u32[]{:S(2)}) copy-start(s32[24]{0:T(128)} %param.12) | copy-start | bytes 292
  7.9 12.3 %copy-start.3 = (f32[6]{0:T(128)S(1)}, f32[6]{0:T(128)}, u32[]{:S(2)}) copy-start(f32[6]{0:T(128)} %constant.41.clone) | copy-start | bytes 76
  7.9 85.4 %copy-start.1 = (f32[32,32,256]{2,1,0:T(8,128)S(1)}, f32[32,32,256]{2,1,0:T(8,128)}, u32[]{:S(2)}) copy-start(f32[32,32,256]{2,1,0:T(8,128)} %get-tuple-element.14.own_ref) | copy-start | bytes 3145732
  7.9 85.4 %all-to-all-start = ((f32[128,6,16,128]{3,2,1,0:T(8,128)}), f32[128,6,16,128]{3,2,1,0:T(8,128)}, u32[]{:S(2)}, u32[]{:S(2)}) async-start(f32[128,6,16,128]{3,2,1,0:T(8,128)} %get-tuple-element.12), calls=%async_computation | async-start | bytes 12582912 | tf_op jit(solution)/shard_map/all_to_all | solution.py:609
  93.3 26.1 %collective-permute-start = (f32[32,32,256]{2,1,0:T(8,128)S(1)}, f32[32,32,256]{2,1,0:T(8,128)S(1)}, u32[]{:S(2)}, u32[]{:S(2)}) collective-permute-start(f32[32,32,256]{2,1,0:T(8,128)S(1)} %copy-done.1), channel_id=1, source_target_pairs={{0,64},{64,0},{1,65},{65,1},{2,66},{66,2},{3,67},{67,3},{4,68},{68... | collective-permute-start | bytes 3145736 | tf_op jit(solution)/shard_map/ppermute | solution.py:635
  119.4 10.0 %copy-start.2 = (f32[32,32,256]{2,1,0:T(8,128)}, f32[32,32,256]{2,1,0:T(8,128)S(1)}, u32[]{:S(2)}) copy-start(f32[32,32,256]{2,1,0:T(8,128)S(1)} %collective-permute-done.partner_ref) | copy-start | bytes 3145732
  119.4 83.5 %all-to-all-start.1 = ((f32[128,6,16,128]{3,2,1,0:T(8,128)}), f32[128,6,16,128]{3,2,1,0:T(8,128)}, u32[]{:S(2)}, u32[]{:S(2)}) async-start(f32[128,6,16,128]{3,2,1,0:T(8,128)} %middle.1), calls=%async_computation.1 | async-start | bytes 12582912 | tf_op jit(solution)/shard_map/all_to_all | solution.py:609

commit v5 on v4

--- a/solution.py
+++ b/solution.py
@@ -144,7 +144,7 @@
     return spec, grid
 
 
-def z_forward(table_hbm, phi_hbm, out_hbm, sq_hbm, table_ref, phi_ref, out_ref, sq_ref, sems):
+def z_forward(table_hbm, phi_hbm, out_hbm, table_ref, phi_ref, out_ref, sems):
     spec, grid = z_pieces(out_hbm, out_ref, phi_hbm, phi_ref, sems)
     steps = groups * 2
     table = pltpu.make_async_copy(table_hbm, table_ref, sems.at[4, 0])
@@ -153,12 +153,10 @@
         for side in range(2):
             grid(step, side, False).start()
     table.wait()
-    sq_ref[...] = jnp.zeros_like(sq_ref)
     rows_ref = phi_ref.reshape(steps * 3072, 128)
     flat_ref = out_ref.reshape(steps * 3072, 128)
 
     def body(step, carry):
-        part_y = step % 2
         for side in range(2):
             grid(step, side, False).wait()
         base = pl.multiple_of(step * 3072, 8)
@@ -184,22 +182,14 @@
                         part * 128 : part * 128 + 128, pair * 128 : pair * 128 + 128
                     ]
         spec(step, True).start()
-        ys = pl.ds(pl.multiple_of(part_y * 16, 16), 16)
-        for side in range(2):
-            lanes = slice(side * 128, side * 128 + 128)
-            one, two = [phi_ref[step, side, v, :, 0:16, :] for v in range(2)]
-            sq_ref[:, ys, lanes] += one * one + two * two
         return carry
 
     lax.fori_loop(0, steps, body, 0)
-    last = pltpu.make_async_copy(sq_ref, sq_hbm, sems.at[3, 0])
-    last.start()
     for step in range(steps):
         spec(step, True).wait()
-    last.wait()
-
-
-def y_there(in_ref, y_ref, left_ref):
+
+
+def y_there(in_ref, y_ref, left_ref, ready=lambda: None):
     lanes = lane_ids(256)
     low_half = lanes < 64
     first_bit = lane_ids(128) // 32 % 2 == 0
@@ -215,8 +205,10 @@
             ]
             evens.append(jnp.where(low_half, first, pltpu.roll(second, 64, 1)))
             odds.append(jnp.where(low_half, pltpu.roll(first, 64, 1), second))
-        even = matmul(left_rows(y_ref[0]), as_right(jnp.concatenate(evens, axis=1)))
-        odd = matmul(left_rows(y_ref[1]), as_right(jnp.concatenate(odds, axis=1)))
+        rights = [as_right(jnp.concatenate(pieces, axis=1)) for pieces in (evens, odds)]
+        if pp == 0:
+            ready()
+        even, odd = [matmul(left_rows(y_ref[side]), rights[side]) for side in range(2)]
         low, high = even + odd, even - odd
         halves.append(
             [
@@ -356,8 +348,8 @@
 
     def part_of(ref, step):
         return ref.at[
-            pl.ds(pl.multiple_of(step % 2 * 64, 64), 64),
-            pl.ds(pl.multiple_of(step // 2 * 2, 2), 2),
+            pl.ds(step % 2 * 64, 64),
+            pl.ds(step // 2 * 2, 2),
         ]
 
     def departure(step):
@@ -376,12 +368,12 @@
         copy.start()
 
     def there_first(step, slot):
-        y_there(part_of(in_ref, step), yf_ref, lefts[slot])
+        ready = copies[0].wait if isinstance(step, int) and step == 0 else lambda: None
+        y_there(part_of(in_ref, step), yf_ref, lefts[slot], ready)
 
     def there_second(step, slot):
         x_there(lefts[slot], xf_ref, fields_of(step))
 
-    copies[0].wait()
     there_first(0, 0)
     copies[1].wait()
 
@@ -453,6 +445,13 @@
         departure(step).wait()
 
 
+def squares(phi_ref, out_ref):
+    total = phi_ref[0] * phi_ref[0]
+    for v in range(1, 2 * groups):
+        total = total + phi_ref[v] * phi_ref[v]
+    out_ref[...] = total
+
+
 def local_part(phi_ref, own_ref, partner_ref, out_ref):
     phi = phi_ref[...]
     total_sq = own_ref[...] + partner_ref[...]
@@ -529,19 +528,31 @@
     return pl.pallas_call(
         z_forward,
         in_specs=[anywhere, anywhere],
-        out_specs=[anywhere, anywhere],
-        out_shape=[hbm((128, 2 * groups, 16, 128)), hbm((32, 32, 256))],
+        out_specs=anywhere,
+        out_shape=hbm((128, 2 * groups, 16, 128)),
         scratch_shapes=[
             pltpu.VMEM(table.shape, jnp.bfloat16),
             pltpu.VMEM((2 * groups, 2, 2, 32, 24, 128), jnp.float32),
             pltpu.VMEM((2 * groups, 128, 3, 8, 128), jnp.float32),
-            pltpu.VMEM((32, 32, 256), jnp.float32),
             pltpu.SemaphoreType.DMA((5, 2 * groups)),
         ],
         compiler_params=pltpu.CompilerParams(vmem_limit_bytes=vmem_bytes),
         cost_estimate=cost(2.4e9, 2 * groups * group_bytes),
         name="z_forward",
     )(table, in_hbm(phi))
+
+
+def call_squares(phi):
+    return pl.pallas_call(
+        squares,
+        grid=(4,),
+        in_specs=[pl.BlockSpec((2 * groups, 32, 8, 256), lambda j: (0, 0, j, 0))],
+        out_specs=pl.BlockSpec((32, 8, 256), lambda j: (0, j, 0)),
+        out_shape=hbm((32, 32, 256)),
+        compiler_params=params(1),
+        cost_estimate=cost(20e6, groups * group_bytes),
+        name="squares",
+    )(in_hbm(phi))
 
 
 def call_local(phi, own, partner):
@@ -558,7 +569,7 @@
         compiler_params=params(2),
         cost_estimate=cost(50e6, 3 * groups * group_bytes),
         name="local_part",
-    )(in_hbm(phi), in_hbm(own), in_hbm(partner))
+    )(in_hbm(phi), in_hbm(own), partner)
 
 
 anywhere = pl.BlockSpec(memory_space=pl.ANY)
@@ -629,14 +640,15 @@
     tables = [in_hbm(jnp.asarray(table)) for table in dft_tables(length)]
     z_fwd, z_inv, y_fwd, y_inv, x_fwd, x_inv = tables
     coefs = coefficients(strains, variant_strain, 12)
-    sent, squares = call_z_forward(order_field, z_fwd)
+    sent, later_field = lax.optimization_barrier((call_z_forward(order_field, z_fwd), order_field))
     arrived = exchange(sent)
-    squares, arrived = lax.optimization_barrier((squares, arrived))
-    partner = lax.ppermute(squares, "var", [(0, 1), (1, 0)])
+    own = call_squares(later_field)
+    own, arrived = lax.optimization_barrier((own, arrived))
+    partner = lax.ppermute(own, "var", [(0, 1), (1, 0)])
     sent = call_middle(coefs, arrived, (y_fwd, x_fwd, x_inv, y_inv))
     sent, partner = lax.optimization_barrier((sent, partner))
     returned = exchange(sent)
-    base = call_local(order_field, squares, partner)
+    base = call_local(order_field, own, partner)
     return call_z_back(returned, base, z_inv)
 
 

time: 212 us -> 211 us (level)
  waiting for transfers between devices: 135 us -> 131 us
  Pallas kernels: 52.9 us -> 55.6 us
    all_to_all x2, waiting for transfers between devices: 135 us -> 131 us  [exchange(): return lax.all_to_all(block, every, split_axis=0, concat_axis=0, tiled=True)]
    pallas_call x1 -> x2, Pallas kernels: 7.83 us -> 11.4 us  [the longest x1 6.81 us: call_z_forward(): pl.pallas_call(z_forward, in_specs=[anywhere, anywhere], out_specs=anywhe...]
  transfers between devices with their start and end apart: 3 -> 3, of which waited for: 2 -> 2; matrix products, arithmetic and copies ran while one was open for 0% -> 0% of each run, Pallas kernels for 17% -> 19%
where the time goes in v5:
time: 211 us; the launch traced here: 210 us
  waiting for transfers between devices  131 us (62%)
  Pallas kernels  55.6 us (26%)
  starting transfers between devices  22.3 us (11%)
    all_to_all x2, waiting for transfers between devices, exchange(): return lax.all_to_all(block, every, split_axis=0, concat_axis=0, tiled=True)  131 us
    pallas_call x1, Pallas kernels, call_middle(): pl.pallas_call(middle, in_specs=[anywhere, inside] + [anywhere] * len(tab...  25.5 us
    all_to_all x2, starting transfers between devices, exchange(): return lax.all_to_all(block, every, split_axis=0, concat_axis=0, tiled=True)  21.9 us
    pallas_call x1, Pallas kernels, call_local(): pl.pallas_call(local_part, grid=(groups, 4), in_specs=[pl.BlockSpec((2, 3...  10.5 us
    pallas_call x1, Pallas kernels, call_z_back(): pl.pallas_call(z_back, in_specs=[anywhere, anywhere, anywhere], out_specs...  8.16 us
    pallas_call x1, Pallas kernels, call_z_forward(): pl.pallas_call(z_forward, in_specs=[anywhere, anywhere], out_specs=anywhe...  6.81 us
    pallas_call x1, Pallas kernels, call_squares(): pl.pallas_call(squares, grid=(4,), in_specs=[pl.BlockSpec((2 * groups, 32...  4.63 us
  transfers between devices with their start and end apart: 3, of which 2 were waited for; matrix products, arithmetic and copies ran while one was open for 0% of the time, Pallas kernels for 19%

profile of v5, /device:TPU:1, one launch (start us, length us, event | category | flops | bytes accessed | tf_op | source)
XLA Modules:
  0.0 209.9 jit_solution(122648031537867575)
XLA Ops:
  0.0 0.0 copy-start
  0.0 6.8 %z_forward.1 = f32[128,6,16,128]{3,2,1,0:T(8,128)} custom-call(bf16[256,512]{1,0:T(8,128)(2,1)} %constant.35.clone.table_hbm, f32[6,32,32,256]{3,2,1,0:T(8,128)} %phi_ref.2), custom_call_target="tpu_custom_call" | custom-call | flops 2400000000 | bytes 12582912 | tf_op jit(solution)/shard_map/z_forward/pallas_call | solution.py:528
  6.8 0.0 copy-start.2
  6.8 11.9 %all-to-all-start = ((f32[128,6,16,128]{3,2,1,0:T(8,128)}), f32[128,6,16,128]{3,2,1,0:T(8,128)}, u32[]{:S(2)}, u32[]{:S(2)}) async-start(f32[128,6,16,128]{3,2,1,0:T(8,128)} %z_forward.1), calls=%async_computation | async-start | bytes 12582912 | tf_op jit(solution)/shard_map/all_to_all | solution.py:620
  18.7 0.0 copy-start.1
  18.8 0.0 copy-done
  18.8 0.0 copy-done.2
  18.8 0.2 fusion
  19.0 0.1 copy.15
  19.1 4.6 %squares.1.own_ref = f32[32,32,256]{2,1,0:T(8,128)} custom-call(f32[6,32,32,256]{3,2,1,0:T(8,128)} %phi_ref.2), custom_call_target="tpu_custom_call" | custom-call | flops 20000000 | bytes 6291456 | tf_op jit(solution)/shard_map/squares/pallas_call | solution.py:546
  23.7 0.0 copy-done.1
  23.7 0.1 multiply_add_fusion
  23.8 0.1 select_maximum_fusion.coef_hbm
  23.9 68.4 %all-to-all-done.in_ref = f32[128,6,16,128]{3,2,1,0:T(8,128)} async-done(((f32[128,6,16,128]{3,2,1,0:T(8,128)}), f32[128,6,16,128]{3,2,1,0:T(8,128)}, u32[]{:S(2)}, u32[]{:S(2)}) %all-to-all-start) | async-done | bytes 6291488 | tf_op jit(solution)/shard_map/all_to_all | solution.py:620
  92.2 0.5 collective-permute-start
  92.7 25.5 %middle.1 = f32[128,6,16,128]{3,2,1,0:T(8,128)} custom-call(f32[13,12]{1,0:T(8,128)S(1)} %select_maximum_fusion.coef_hbm, f32[128,6,16,128]{3,2,1,0:T(8,128)} %all-to-all-done.in_ref, bf16[2,256,512]{2,1,0:T(8,128)(2,1)} %constant.37.clone.yf_hbm, bf16[2,512,256]{2,1,0:T(8,128)(2,1)} %constant.39.clone.xf_hbm, bf16[2,512,256]{2,1,0:T(8,128)(2,1)} %constant.40.clone.xb_hbm, ...), custom_call_target="tpu_custom_call" | custom-call | flops 20000000000 | bytes 37748736 | tf_op jit(solution)/shard_map/middle/pallas_call | solution.py:589
  118.2 0.0 collective-permute-done.partner_ref
  118.2 10.0 %all-to-all-start.1 = ((f32[128,6,16,128]{3,2,1,0:T(8,128)}), f32[128,6,16,128]{3,2,1,0:T(8,128)}, u32[]{:S(2)}, u32[]{:S(2)}) async-start(f32[128,6,16,128]{3,2,1,0:T(8,128)} %middle.1), calls=%async_computation.1 | async-start | bytes 12582912 | tf_op jit(solution)/shard_map/all_to_all | solution.py:620
  128.2 10.5 %local_part.1.base_hbm = f32[6,32,32,256]{3,2,1,0:T(8,128)} custom-call(f32[6,32,32,256]{3,2,1,0:T(8,128)} %phi_ref.2, f32[32,32,256]{2,1,0:T(8,128)} %squares.1.own_ref, f32[32,32,256]{2,1,0:T(8,128)S(1)} %collective-permute-done.partner_ref), custom_call_target="tpu_custom_call" | custom-call | flops 50000000 | bytes 18874368 | tf_op jit(solution)/shard_map/local_part/pallas_call | solution.py:559
  138.7 63.0 %all-to-all-done.1.spec_hbm = f32[128,6,16,128]{3,2,1,0:T(8,128)} async-done(((f32[128,6,16,128]{3,2,1,0:T(8,128)}), f32[128,6,16,128]{3,2,1,0:T(8,128)}, u32[]{:S(2)}, u32[]{:S(2)}) %all-to-all-start.1) | async-done | bytes 6291488 | tf_op jit(solution)/shard_map/all_to_all | solution.py:620
  201.7 8.2 %z_back.1 = f32[6,32,32,256]{3,2,1,0:T(8,128)} custom-call(bf16[512,256]{1,0:T(8,128)(2,1)} %constant.36.clone.table_hbm, f32[128,6,16,128]{3,2,1,0:T(8,128)} %all-to-all-done.1.spec_hbm, f32[6,32,32,256]{3,2,1,0:T(8,128)} %local_part.1.base_hbm), custom_call_target="tpu_custom_call" | custom-call | flops 2400000000 | bytes 18874368 | tf_op jit(solution)/shard_map/z_back/pallas_call | solution.py:602
  (1 shorter events, 0.0 us)
Async XLA Ops:
  0.0 18.8 %copy-start = (f32[24,6]{0,1:T(8,128)S(1)}, f32[24,6]{0,1:T(8,128)}, u32[]{:S(2)}) copy-start(f32[24,6]{0,1:T(8,128)} %param.11) | copy-start | bytes 1732
  6.8 12.0 %copy-start.2 = (s32[24]{0:T(128)S(1)}, s32[24]{0:T(128)}, u32[]{:S(2)}) copy-start(s32[24]{0:T(128)} %param.12) | copy-start | bytes 292
  6.8 85.4 %all-to-all-start = ((f32[128,6,16,128]{3,2,1,0:T(8,128)}), f32[128,6,16,128]{3,2,1,0:T(8,128)}, u32[]{:S(2)}, u32[]{:S(2)}) async-start(f32[128,6,16,128]{3,2,1,0:T(8,128)} %z_forward.1), calls=%async_computation | async-start | bytes 12582912 | tf_op jit(solution)/shard_map/all_to_all | solution.py:620
  18.7 5.0 %copy-start.1 = (f32[6]{0:T(128)S(1)}, f32[6]{0:T(128)}, u32[]{:S(2)}) copy-start(f32[6]{0:T(128)} %constant.41.clone) | copy-start | bytes 76
  92.2 26.0 %collective-permute-start = (f32[32,32,256]{2,1,0:T(8,128)}, f32[32,32,256]{2,1,0:T(8,128)S(1)}, u32[]{:S(2)}, u32[]{:S(2)}) collective-permute-start(f32[32,32,256]{2,1,0:T(8,128)} %squares.1.own_ref), channel_id=1, source_target_pairs={{0,64},{64,0},{1,65},{65,1},{2,66},{66,2},{3,67},{67,3},{4,68},{68... | collective-permute-start | bytes 3145736 | tf_op jit(solution)/shard_map/ppermute | solution.py:647
  118.2 83.5 %all-to-all-start.1 = ((f32[128,6,16,128]{3,2,1,0:T(8,128)}), f32[128,6,16,128]{3,2,1,0:T(8,128)}, u32[]{:S(2)}, u32[]{:S(2)}) async-start(f32[128,6,16,128]{3,2,1,0:T(8,128)} %middle.1), calls=%async_computation.1 | async-start | bytes 12582912 | tf_op jit(solution)/shard_map/all_to_all | solution.py:620

commit v6 on v5

--- a/solution.py
+++ b/solution.py
@@ -153,8 +153,8 @@
         for side in range(2):
             grid(step, side, False).start()
     table.wait()
-    rows_ref = phi_ref.reshape(steps * 3072, 128)
-    flat_ref = out_ref.reshape(steps * 3072, 128)
+    rows_ref = phi_ref.reshape((steps + 1) * 3072, 128)
+    flat_ref = out_ref.reshape((steps + 1) * 3072, 128)
 
     def body(step, carry):
         for side in range(2):
@@ -471,8 +471,8 @@
         if step == 0:
             table.start()
     table.wait()
-    flat_ref = spec_ref.reshape(steps * 3072, 128)
-    rows_ref = base_ref.reshape(steps * 3072, 128)
+    flat_ref = spec_ref.reshape((steps + 1) * 3072, 128)
+    rows_ref = base_ref.reshape((steps + 1) * 3072, 128)
 
     def body(step, carry):
         base = pl.multiple_of(step * 3072, 8)
@@ -532,8 +532,8 @@
         out_shape=hbm((128, 2 * groups, 16, 128)),
         scratch_shapes=[
             pltpu.VMEM(table.shape, jnp.bfloat16),
-            pltpu.VMEM((2 * groups, 2, 2, 32, 24, 128), jnp.float32),
-            pltpu.VMEM((2 * groups, 128, 3, 8, 128), jnp.float32),
+            pltpu.VMEM((2 * groups + 1, 2, 2, 32, 24, 128), jnp.float32),
+            pltpu.VMEM((2 * groups + 1, 128, 3, 8, 128), jnp.float32),
             pltpu.SemaphoreType.DMA((5, 2 * groups)),
         ],
         compiler_params=pltpu.CompilerParams(vmem_limit_bytes=vmem_bytes),
@@ -606,8 +606,8 @@
         out_shape=hbm(base.shape),
         scratch_shapes=[
             pltpu.VMEM(table.shape, jnp.bfloat16),
-            pltpu.VMEM((2 * groups, 128, 3, 8, 128), jnp.float32),
-            pltpu.VMEM((2 * groups, 2, 2, 32, 24, 128), jnp.float32),
+            pltpu.VMEM((2 * groups + 1, 128, 3, 8, 128), jnp.float32),
+            pltpu.VMEM((2 * groups + 1, 2, 2, 32, 24, 128), jnp.float32),
             pltpu.SemaphoreType.DMA((6, 2 * groups)),
         ],
         compiler_params=pltpu.CompilerParams(vmem_limit_bytes=vmem_bytes),

time: 211 us -> 211 us (level)
  no operation moved by 1% of the time
where the time goes in v6:
time: 211 us; the launch traced here: 210 us
  waiting for transfers between devices  131 us (62%)
  Pallas kernels  55.6 us (26%)
  starting transfers between devices  22.3 us (11%)
    all_to_all x2, waiting for transfers between devices, exchange(): return lax.all_to_all(block, every, split_axis=0, concat_axis=0, tiled=True)  131 us
    pallas_call x1, Pallas kernels, call_middle(): pl.pallas_call(middle, in_specs=[anywhere, inside] + [anywhere] * len(tab...  25.5 us
    all_to_all x2, starting transfers between devices, exchange(): return lax.all_to_all(block, every, split_axis=0, concat_axis=0, tiled=True)  21.9 us
    pallas_call x1, Pallas kernels, call_local(): pl.pallas_call(local_part, grid=(groups, 4), in_specs=[pl.BlockSpec((2, 3...  10.5 us
    pallas_call x1, Pallas kernels, call_z_back(): pl.pallas_call(z_back, in_specs=[anywhere, anywhere, anywhere], out_specs...  8.16 us
    pallas_call x1, Pallas kernels, call_z_forward(): pl.pallas_call(z_forward, in_specs=[anywhere, anywhere], out_specs=anywhe...  6.81 us
    pallas_call x1, Pallas kernels, call_squares(): pl.pallas_call(squares, grid=(4,), in_specs=[pl.BlockSpec((2 * groups, 32...  4.63 us
  transfers between devices with their start and end apart: 3, of which 2 were waited for; matrix products, arithmetic and copies ran while one was open for 0% of the time, Pallas kernels for 19%

profile of v6, /device:TPU:1, one launch (start us, length us, event | category | flops | bytes accessed | tf_op | source)
XLA Modules:
  0.0 209.9 jit_solution(14052091624450780741)
XLA Ops:
  0.0 0.0 copy-start
  0.0 6.8 %z_forward.1 = f32[128,6,16,128]{3,2,1,0:T(8,128)} custom-call(bf16[256,512]{1,0:T(8,128)(2,1)} %constant.35.clone.table_hbm, f32[6,32,32,256]{3,2,1,0:T(8,128)} %phi_ref.2), custom_call_target="tpu_custom_call" | custom-call | flops 2400000000 | bytes 12582912 | tf_op jit(solution)/shard_map/z_forward/pallas_call | solution.py:528
  6.8 0.0 copy-start.2
  6.8 11.9 %all-to-all-start = ((f32[128,6,16,128]{3,2,1,0:T(8,128)}), f32[128,6,16,128]{3,2,1,0:T(8,128)}, u32[]{:S(2)}, u32[]{:S(2)}) async-start(f32[128,6,16,128]{3,2,1,0:T(8,128)} %z_forward.1), calls=%async_computation | async-start | bytes 12582912 | tf_op jit(solution)/shard_map/all_to_all | solution.py:620
  18.7 0.0 copy-start.1
  18.8 0.0 copy-done
  18.8 0.0 copy-done.2
  18.8 0.2 fusion
  19.0 0.1 copy.15
  19.1 4.6 %squares.1.own_ref = f32[32,32,256]{2,1,0:T(8,128)} custom-call(f32[6,32,32,256]{3,2,1,0:T(8,128)} %phi_ref.2), custom_call_target="tpu_custom_call" | custom-call | flops 20000000 | bytes 6291456 | tf_op jit(solution)/shard_map/squares/pallas_call | solution.py:546
  23.7 0.0 copy-done.1
  23.7 0.1 multiply_add_fusion
  23.8 0.1 select_maximum_fusion.coef_hbm
  23.9 68.4 %all-to-all-done.in_ref = f32[128,6,16,128]{3,2,1,0:T(8,128)} async-done(((f32[128,6,16,128]{3,2,1,0:T(8,128)}), f32[128,6,16,128]{3,2,1,0:T(8,128)}, u32[]{:S(2)}, u32[]{:S(2)}) %all-to-all-start) | async-done | bytes 6291488 | tf_op jit(solution)/shard_map/all_to_all | solution.py:620
  92.2 0.5 collective-permute-start
  92.7 25.5 %middle.1 = f32[128,6,16,128]{3,2,1,0:T(8,128)} custom-call(f32[13,12]{1,0:T(8,128)S(1)} %select_maximum_fusion.coef_hbm, f32[128,6,16,128]{3,2,1,0:T(8,128)} %all-to-all-done.in_ref, bf16[2,256,512]{2,1,0:T(8,128)(2,1)} %constant.37.clone.yf_hbm, bf16[2,512,256]{2,1,0:T(8,128)(2,1)} %constant.39.clone.xf_hbm, bf16[2,512,256]{2,1,0:T(8,128)(2,1)} %constant.40.clone.xb_hbm, ...), custom_call_target="tpu_custom_call" | custom-call | flops 20000000000 | bytes 37748736 | tf_op jit(solution)/shard_map/middle/pallas_call | solution.py:589
  118.2 0.0 collective-permute-done.partner_ref
  118.2 10.0 %all-to-all-start.1 = ((f32[128,6,16,128]{3,2,1,0:T(8,128)}), f32[128,6,16,128]{3,2,1,0:T(8,128)}, u32[]{:S(2)}, u32[]{:S(2)}) async-start(f32[128,6,16,128]{3,2,1,0:T(8,128)} %middle.1), calls=%async_computation.1 | async-start | bytes 12582912 | tf_op jit(solution)/shard_map/all_to_all | solution.py:620
  128.2 10.5 %local_part.1.base_hbm = f32[6,32,32,256]{3,2,1,0:T(8,128)} custom-call(f32[6,32,32,256]{3,2,1,0:T(8,128)} %phi_ref.2, f32[32,32,256]{2,1,0:T(8,128)} %squares.1.own_ref, f32[32,32,256]{2,1,0:T(8,128)S(1)} %collective-permute-done.partner_ref), custom_call_target="tpu_custom_call" | custom-call | flops 50000000 | bytes 18874368 | tf_op jit(solution)/shard_map/local_part/pallas_call | solution.py:559
  138.7 63.0 %all-to-all-done.1.spec_hbm = f32[128,6,16,128]{3,2,1,0:T(8,128)} async-done(((f32[128,6,16,128]{3,2,1,0:T(8,128)}), f32[128,6,16,128]{3,2,1,0:T(8,128)}, u32[]{:S(2)}, u32[]{:S(2)}) %all-to-all-start.1) | async-done | bytes 6291488 | tf_op jit(solution)/shard_map/all_to_all | solution.py:620
  201.7 8.2 %z_back.1 = f32[6,32,32,256]{3,2,1,0:T(8,128)} custom-call(bf16[512,256]{1,0:T(8,128)(2,1)} %constant.36.clone.table_hbm, f32[128,6,16,128]{3,2,1,0:T(8,128)} %all-to-all-done.1.spec_hbm, f32[6,32,32,256]{3,2,1,0:T(8,128)} %local_part.1.base_hbm), custom_call_target="tpu_custom_call" | custom-call | flops 2400000000 | bytes 18874368 | tf_op jit(solution)/shard_map/z_back/pallas_call | solution.py:602
  (1 shorter events, 0.0 us)
Async XLA Ops:
  0.0 18.8 %copy-start = (f32[24,6]{0,1:T(8,128)S(1)}, f32[24,6]{0,1:T(8,128)}, u32[]{:S(2)}) copy-start(f32[24,6]{0,1:T(8,128)} %param.11) | copy-start | bytes 1732
  6.8 12.0 %copy-start.2 = (s32[24]{0:T(128)S(1)}, s32[24]{0:T(128)}, u32[]{:S(2)}) copy-start(s32[24]{0:T(128)} %param.12) | copy-start | bytes 292
  6.8 85.4 %all-to-all-start = ((f32[128,6,16,128]{3,2,1,0:T(8,128)}), f32[128,6,16,128]{3,2,1,0:T(8,128)}, u32[]{:S(2)}, u32[]{:S(2)}) async-start(f32[128,6,16,128]{3,2,1,0:T(8,128)} %z_forward.1), calls=%async_computation | async-start | bytes 12582912 | tf_op jit(solution)/shard_map/all_to_all | solution.py:620
  18.7 5.0 %copy-start.1 = (f32[6]{0:T(128)S(1)}, f32[6]{0:T(128)}, u32[]{:S(2)}) copy-start(f32[6]{0:T(128)} %constant.41.clone) | copy-start | bytes 76
  92.2 26.0 %collective-permute-start = (f32[32,32,256]{2,1,0:T(8,128)}, f32[32,32,256]{2,1,0:T(8,128)S(1)}, u32[]{:S(2)}, u32[]{:S(2)}) collective-permute-start(f32[32,32,256]{2,1,0:T(8,128)} %squares.1.own_ref), channel_id=1, source_target_pairs={{0,64},{64,0},{1,65},{65,1},{2,66},{66,2},{3,67},{67,3},{4,68},{68... | collective-permute-start | bytes 3145736 | tf_op jit(solution)/shard_map/ppermute | solution.py:647
  118.2 83.5 %all-to-all-start.1 = ((f32[128,6,16,128]{3,2,1,0:T(8,128)}), f32[128,6,16,128]{3,2,1,0:T(8,128)}, u32[]{:S(2)}, u32[]{:S(2)}) async-start(f32[128,6,16,128]{3,2,1,0:T(8,128)} %middle.1), calls=%async_computation.1 | async-start | bytes 12582912 | tf_op jit(solution)/shard_map/all_to_all | solution.py:620

commit v7 on v6

--- a/solution.py
+++ b/solution.py
@@ -106,6 +106,12 @@
 def right_rows(table):
     depth = table.shape[0] // 2
     return jnp.concatenate([table[:depth], table], axis=0)
+
+
+def y_product(table, value):
+    high, low = split_value(value)
+    both = matmul(jnp.concatenate([table[:, :256], table[:, 256:]], axis=0), high)
+    return both[:256] + both[256:] + matmul(table[:, :256], low)
 
 
 def matmul(left, right):
@@ -270,7 +276,7 @@
         results = []
         for parity, pieces in enumerate((evens, odds)):
             right = jnp.concatenate([jnp.concatenate(p, axis=0) for p in pieces], axis=1)
-            results.append(matmul(left_rows(y_ref[parity]), as_right(right)))
+            results.append(y_product(y_ref[parity], right))
         for pp in range(2):
             even = results[0][:, pp * 128 : pp * 128 + 128]
             odd = results[1][:, pp * 128 : pp * 128 + 128]
@@ -418,7 +424,7 @@
             field_ref[place, rows, :] = total
         return carry
 
-    lax.fori_loop(0, length // 8, tile, 0)
+    lax.fori_loop(0, length // 8, tile, 0, unroll=2)
     copies[2].wait()
     copies[3].wait()
 

time: 211 us -> 210 us (level)
  no operation moved by 1% of the time
where the time goes in v7:
time: 210 us; the launch traced here: 209 us
  waiting for transfers between devices  131 us (62%)
  Pallas kernels  55.2 us (26%)
  starting transfers between devices  22.3 us (11%)
    all_to_all x2, waiting for transfers between devices, exchange(): return lax.all_to_all(block, every, split_axis=0, concat_axis=0, tiled=True)  131 us
    pallas_call x1, Pallas kernels, call_middle(): pl.pallas_call(middle, in_specs=[anywhere, inside] + [anywhere] * len(tab...  25.1 us
    all_to_all x2, starting transfers between devices, exchange(): return lax.all_to_all(block, every, split_axis=0, concat_axis=0, tiled=True)  21.9 us
    pallas_call x1, Pallas kernels, call_local(): pl.pallas_call(local_part, grid=(groups, 4), in_specs=[pl.BlockSpec((2, 3...  10.5 us
    pallas_call x1, Pallas kernels, call_z_back(): pl.pallas_call(z_back, in_specs=[anywhere, anywhere, anywhere], out_specs...  8.16 us
    pallas_call x1, Pallas kernels, call_z_forward(): pl.pallas_call(z_forward, in_specs=[anywhere, anywhere], out_specs=anywhe...  6.81 us
    pallas_call x1, Pallas kernels, call_squares(): pl.pallas_call(squares, grid=(4,), in_specs=[pl.BlockSpec((2 * groups, 32...  4.63 us
  transfers between devices with their start and end apart: 3, of which 2 were waited for; matrix products, arithmetic and copies ran while one was open for 0% of the time, Pallas kernels for 19%

profile of v7, /device:TPU:1, one launch (start us, length us, event | category | flops | bytes accessed | tf_op | source)
XLA Modules:
  0.0 209.5 jit_solution(15369217794288177943)
XLA Ops:
  0.0 0.0 copy-start
  0.0 6.8 %z_forward.1 = f32[128,6,16,128]{3,2,1,0:T(8,128)} custom-call(bf16[256,512]{1,0:T(8,128)(2,1)} %constant.35.clone.table_hbm, f32[6,32,32,256]{3,2,1,0:T(8,128)} %phi_ref.2), custom_call_target="tpu_custom_call" | custom-call | flops 2400000000 | bytes 12582912 | tf_op jit(solution)/shard_map/z_forward/pallas_call | solution.py:534
  6.8 0.0 copy-start.2
  6.8 11.9 %all-to-all-start = ((f32[128,6,16,128]{3,2,1,0:T(8,128)}), f32[128,6,16,128]{3,2,1,0:T(8,128)}, u32[]{:S(2)}, u32[]{:S(2)}) async-start(f32[128,6,16,128]{3,2,1,0:T(8,128)} %z_forward.1), calls=%async_computation | async-start | bytes 12582912 | tf_op jit(solution)/shard_map/all_to_all | solution.py:626
  18.7 0.0 copy-start.1
  18.8 0.0 copy-done
  18.8 0.0 copy-done.2
  18.8 0.2 fusion
  19.0 0.1 copy.15
  19.1 4.6 %squares.1.own_ref = f32[32,32,256]{2,1,0:T(8,128)} custom-call(f32[6,32,32,256]{3,2,1,0:T(8,128)} %phi_ref.2), custom_call_target="tpu_custom_call" | custom-call | flops 20000000 | bytes 6291456 | tf_op jit(solution)/shard_map/squares/pallas_call | solution.py:552
  23.7 0.0 copy-done.1
  23.7 0.1 multiply_add_fusion
  23.8 0.1 select_maximum_fusion.coef_hbm
  23.9 68.4 %all-to-all-done.in_ref = f32[128,6,16,128]{3,2,1,0:T(8,128)} async-done(((f32[128,6,16,128]{3,2,1,0:T(8,128)}), f32[128,6,16,128]{3,2,1,0:T(8,128)}, u32[]{:S(2)}, u32[]{:S(2)}) %all-to-all-start) | async-done | bytes 6291488 | tf_op jit(solution)/shard_map/all_to_all | solution.py:626
  92.2 0.5 collective-permute-start
  92.7 25.1 %middle.1 = f32[128,6,16,128]{3,2,1,0:T(8,128)} custom-call(f32[13,12]{1,0:T(8,128)S(1)} %select_maximum_fusion.coef_hbm, f32[128,6,16,128]{3,2,1,0:T(8,128)} %all-to-all-done.in_ref, bf16[2,256,512]{2,1,0:T(8,128)(2,1)} %constant.37.clone.yf_hbm, bf16[2,512,256]{2,1,0:T(8,128)(2,1)} %constant.39.clone.xf_hbm, bf16[2,512,256]{2,1,0:T(8,128)(2,1)} %constant.40.clone.xb_hbm, ...), custom_call_target="tpu_custom_call" | custom-call | flops 20000000000 | bytes 37748736 | tf_op jit(solution)/shard_map/middle/pallas_call | solution.py:595
  117.8 0.0 collective-permute-done.partner_ref
  117.8 10.0 %all-to-all-start.1 = ((f32[128,6,16,128]{3,2,1,0:T(8,128)}), f32[128,6,16,128]{3,2,1,0:T(8,128)}, u32[]{:S(2)}, u32[]{:S(2)}) async-start(f32[128,6,16,128]{3,2,1,0:T(8,128)} %middle.1), calls=%async_computation.1 | async-start | bytes 12582912 | tf_op jit(solution)/shard_map/all_to_all | solution.py:626
  127.8 10.5 %local_part.1.base_hbm = f32[6,32,32,256]{3,2,1,0:T(8,128)} custom-call(f32[6,32,32,256]{3,2,1,0:T(8,128)} %phi_ref.2, f32[32,32,256]{2,1,0:T(8,128)} %squares.1.own_ref, f32[32,32,256]{2,1,0:T(8,128)S(1)} %collective-permute-done.partner_ref), custom_call_target="tpu_custom_call" | custom-call | flops 50000000 | bytes 18874368 | tf_op jit(solution)/shard_map/local_part/pallas_call | solution.py:565
  138.3 63.0 %all-to-all-done.1.spec_hbm = f32[128,6,16,128]{3,2,1,0:T(8,128)} async-done(((f32[128,6,16,128]{3,2,1,0:T(8,128)}), f32[128,6,16,128]{3,2,1,0:T(8,128)}, u32[]{:S(2)}, u32[]{:S(2)}) %all-to-all-start.1) | async-done | bytes 6291488 | tf_op jit(solution)/shard_map/all_to_all | solution.py:626
  201.3 8.2 %z_back.1 = f32[6,32,32,256]{3,2,1,0:T(8,128)} custom-call(bf16[512,256]{1,0:T(8,128)(2,1)} %constant.36.clone.table_hbm, f32[128,6,16,128]{3,2,1,0:T(8,128)} %all-to-all-done.1.spec_hbm, f32[6,32,32,256]{3,2,1,0:T(8,128)} %local_part.1.base_hbm), custom_call_target="tpu_custom_call" | custom-call | flops 2400000000 | bytes 18874368 | tf_op jit(solution)/shard_map/z_back/pallas_call | solution.py:608
  (1 shorter events, 0.0 us)
Async XLA Ops:
  0.0 18.8 %copy-start = (f32[24,6]{0,1:T(8,128)S(1)}, f32[24,6]{0,1:T(8,128)}, u32[]{:S(2)}) copy-start(f32[24,6]{0,1:T(8,128)} %param.11) | copy-start | bytes 1732
  6.8 12.0 %copy-start.2 = (s32[24]{0:T(128)S(1)}, s32[24]{0:T(128)}, u32[]{:S(2)}) copy-start(s32[24]{0:T(128)} %param.12) | copy-start | bytes 292
  6.8 85.4 %all-to-all-start = ((f32[128,6,16,128]{3,2,1,0:T(8,128)}), f32[128,6,16,128]{3,2,1,0:T(8,128)}, u32[]{:S(2)}, u32[]{:S(2)}) async-start(f32[128,6,16,128]{3,2,1,0:T(8,128)} %z_forward.1), calls=%async_computation | async-start | bytes 12582912 | tf_op jit(solution)/shard_map/all_to_all | solution.py:626
  18.7 5.0 %copy-start.1 = (f32[6]{0:T(128)S(1)}, f32[6]{0:T(128)}, u32[]{:S(2)}) copy-start(f32[6]{0:T(128)} %constant.41.clone) | copy-start | bytes 76
  92.2 25.5 %collective-permute-start = (f32[32,32,256]{2,1,0:T(8,128)}, f32[32,32,256]{2,1,0:T(8,128)S(1)}, u32[]{:S(2)}, u32[]{:S(2)}) collective-permute-start(f32[32,32,256]{2,1,0:T(8,128)} %squares.1.own_ref), channel_id=1, source_target_pairs={{0,64},{64,0},{1,65},{65,1},{2,66},{66,2},{3,67},{67,3},{4,68},{68... | collective-permute-start | bytes 3145736 | tf_op jit(solution)/shard_map/ppermute | solution.py:653
  117.8 83.5 %all-to-all-start.1 = ((f32[128,6,16,128]{3,2,1,0:T(8,128)}), f32[128,6,16,128]{3,2,1,0:T(8,128)}, u32[]{:S(2)}, u32[]{:S(2)}) async-start(f32[128,6,16,128]{3,2,1,0:T(8,128)} %middle.1), calls=%async_computation.1 | async-start | bytes 12582912 | tf_op jit(solution)/shard_map/all_to_all | solution.py:626
